TPU v7x, 256 devices: a whole 4x4x8 slice. The times are simulated.
256 devices in a mesh: rep: 2 (over core), shard: 128 (over y, x, z).
Axes of the slice: x: 4, y: 4, z: 8, core: 2. Of those that a mesh axis runs over, the one named last changes fastest.
Arguments:
- gradients: float32 [2, 88, 1024, 1024], P('rep', None, 'shard'), may hold values from -0.2 to 0.2
- left_stats: float32 [88, 1024, 1024], P(None, 'shard', 'rep'), may hold values from -0.09 to 4
- right_stats: float32 [88, 1024, 1024], P(None, 'shard', 'rep'), may hold values from -0.09 to 4
- left_root: bfloat16 [128, 2, 1024, 1024], P('shard', None, None, 'rep'), may hold values from -0.07 to 8, as said below
- right_root: bfloat16 [128, 2, 1024, 1024], P('shard', None, None, 'rep'), may hold values from -0.07 to 8, as said below
- block_owner: int32 [88], replicated, may hold values from 0 to 127, as said below
Outputs:
- left_new: float32 [88, 1024, 1024], P(None, 'shard', 'rep')
- right_new: float32 [88, 1024, 1024], P(None, 'shard', 'rep')
- update: bfloat16 [88, 1024, 1024], P(None, 'shard', 'rep')
Inputs may be any that keep to these rules, and one draw needn't show every extreme that they name: `block_owner`: each owner is named by at most 2 blocks; 32 owners are named by exactly two blocks and 24 by exactly one. `left_root`: entry [o, j] belongs to the block that comes j-th, counting from 0 by block index, among those owned by o; entries that no block takes are never read. `right_root`: laid out as left_root.
All inputs are finite; a program needn't handle non-finite values.
Results may differ from a plain program's by a relative error of at most 0.006.
Values may be sent and summed in bfloat16 or wider, within the bound.
No kernel may reach another device: no remote copies, remote signals or barrier semaphores. Data moves between devices by JAX's collectives and lax.ppermute only.
A program may use at most 128 MiB of HBM per device.

v0:
```python
from functools import partial

import jax
import jax.numpy as jnp
from jax import lax
from jax.sharding import PartitionSpec as P


def swapped(value, axis, apart):
    return lax.ppermute(value, axis, [(i, i ^ 1 << apart) for i in range(lax.axis_size(axis))])


def owner_table(block_owner, owners, slot_count):
    block_count = block_owner.shape[0]
    owner_match = (block_owner[:, None] == jnp.arange(owners, dtype=jnp.int32)[None, :]).astype(
        jnp.int32
    )
    earlier = jnp.cumsum(owner_match, axis=0) - owner_match
    slot_of = jnp.sum(earlier * owner_match, axis=1)
    held = jnp.sum(owner_match, axis=0)
    table_pos = slot_of * owners + block_owner
    positions = jnp.arange(owners * slot_count, dtype=jnp.int32)
    pos_match = (table_pos[:, None] == positions[None, :]).astype(jnp.int32)
    block_ids = jnp.arange(block_count, dtype=jnp.int32)
    source = (
        jnp.sum(pos_match * block_ids[:, None], axis=0)
        + (1 - jnp.sum(pos_match, axis=0)) * block_count
    )
    return (table_pos, source, held)


def join_halves(mine, other, core_side):
    first = jnp.where(core_side == 0, mine, other)
    second = jnp.where(core_side == 0, other, mine)
    return jnp.concatenate([first, second], axis=-1)


def block_work(full_grad, left_full, right_cols, core_side, half_width):
    grad_rows = lax.dynamic_slice_in_dim(full_grad, core_side * half_width, half_width, 0)
    grad_cols = lax.dynamic_slice_in_dim(full_grad, core_side * half_width, half_width, 1)
    left_gram = lax.dot_general(
        full_grad, grad_rows, (((1,), (1,)), ((), ())), preferred_element_type=jnp.float32
    )
    right_gram = lax.dot_general(
        full_grad, grad_cols, (((0,), (0,)), ((), ())), preferred_element_type=jnp.float32
    )
    applied = jnp.dot(full_grad, right_cols, preferred_element_type=jnp.float32).astype(
        jnp.bfloat16
    )
    update_cols = jnp.dot(left_full, applied, preferred_element_type=jnp.float32).astype(
        jnp.bfloat16
    )
    return (left_gram, right_gram, update_cols)


def per_device(gradients, left_stats, right_stats, left_root, right_root, block_owner):
    owners = lax.axis_size("shard")
    slot_count = left_root.shape[1]
    block_count, share_rows, half_width = left_stats.shape
    full_width = 2 * half_width
    core_side = lax.axis_index("rep")
    table_pos, source, held = owner_table(block_owner, owners, slot_count)
    replica_total = lax.psum(gradients[0], "rep")
    grad_share = replica_total.astype(jnp.bfloat16)
    blank = jnp.zeros((1, share_rows, full_width), jnp.bfloat16)
    outgoing = jnp.concatenate([grad_share, blank], axis=0)[source]
    outgoing = outgoing.reshape(slot_count, owners, share_rows, full_width)
    arrived = lax.all_to_all(outgoing, "shard", split_axis=1, concat_axis=1, tiled=True)
    full_grads = arrived.reshape(slot_count, owners * share_rows, full_width)
    other_left = swapped(left_root[0], "rep", 0)
    left_fulls = join_halves(left_root[0], other_left, core_side)
    working = partial(block_work, half_width=half_width)
    gram_left = []
    gram_right = []
    new_blocks = []
    for slot_index in range(slot_count):
        operands = (
            full_grads[slot_index],
            left_fulls[slot_index],
            right_root[0, slot_index],
            core_side,
        )
        results = working(*operands)
        gram_left.append(results[0])
        gram_right.append(results[1])
        new_blocks.append(results[2])
    owner_shape = (slot_count, owners, share_rows, half_width)
    left_back, right_back = (
        lax.all_to_all(
            jnp.stack(gram_left).reshape(owner_shape).astype(jnp.bfloat16),
            "shard",
            split_axis=1,
            concat_axis=1,
            tiled=True,
        ).astype(jnp.float32),
        lax.all_to_all(
            jnp.stack(gram_right).reshape(owner_shape).astype(jnp.bfloat16),
            "shard",
            split_axis=1,
            concat_axis=1,
            tiled=True,
        ).astype(jnp.float32),
    )
    update_back = lax.all_to_all(
        jnp.stack(new_blocks).reshape(owner_shape), "shard", split_axis=1, concat_axis=1, tiled=True
    )
    flat_shape = (slot_count * owners, share_rows, half_width)
    left_new = left_stats + left_back.reshape(flat_shape)[table_pos]
    right_new = right_stats + right_back.reshape(flat_shape)[table_pos]
    update = update_back.reshape(flat_shape)[table_pos]
    return (left_new, right_new, update)


def solution(mesh):
    return jax.shard_map(
        per_device,
        mesh=mesh,
        in_specs=(
            P("rep", None, "shard", None),
            P(None, "shard", "rep"),
            P(None, "shard", "rep"),
            P("shard", None, None, "rep"),
            P("shard", None, None, "rep"),
            P(),
        ),
        out_specs=(P(None, "shard", "rep"), P(None, "shard", "rep"), P(None, "shard", "rep")),
        check_vma=False,
    )
```

profile of v0, /device:TPU:32, one launch (start us, length us, event | category | flops | bytes accessed | tf_op | source)
XLA Modules:
  0.0 333.1 jit_solution(13182010022138579288)
XLA Ops:
  0.6 0.7 fusion.58
  1.4 0.1 reduce_window_sum.11
  1.5 0.8 select_reduce_fusion.1
  2.3 0.7 compare_select_fusion.1
  3.0 0.1 convert_reduce_fusion
  3.1 11.6 %all-reduce.2 = bf16[88,8,1024]{2,1,0:T(8,128)(2,1)S(1)} all-reduce(f32[88,8,1024]{2,1,0:T(8,128)} %bitcast.106), channel_id=1, replica_groups=mesh['rep'=2,'shard'=128] {'rep'}, use_global_device_ids=true, to_apply=%region_0.0 | all-reduce | flops 720896 | bytes 4325376 | tf_op jit(solution)/shard_map/psum | solution.py:63
  14.7 0.1 concatenate.11
  14.8 2.8 gather_fusion
  17.6 4.8 %copy.37 = bf16[2,128,8,1024]{3,2,0,1:T(8,128)(2,1)} copy(bf16[2,128,8,1024]{3,2,1,0:T(8,128)(2,1)} %bitcast.104) | data formatting | bytes 8388608 | tf_op jit(solution)/shard_map/reshape | solution.py:67
  22.4 0.0 copy-start.1
  22.4 15.6 %all-to-all-start = ((bf16[2,128,8,1024]{3,2,0,1:T(8,128)(2,1)}), bf16[2,128,8,1024]{3,2,0,1:T(8,128)(2,1)}, u32[]{:S(2)}, u32[]{:S(2)}) async-start(bf16[2,128,8,1024]{3,2,0,1:T(8,128)(2,1)} %copy.37), calls=%async_computation | async-start | bytes 8388608 | tf_op jit(solution)/shard_map/all_to_all | solution.py:68
  38.0 0.0 copy-done.1
  38.0 0.1 collective-permute-start
  38.1 4.3 %collective-permute-done = bf16[2,1024,512]{2,1,0:T(8,128)(2,1)} collective-permute-done((bf16[2,1024,512]{2,1,0:T(8,128)(2,1)S(1)}, bf16[2,1024,512]{2,1,0:T(8,128)(2,1)}, u32[]{:S(2)}, u32[]{:S(2)}) %collective-permute-start) | collective-permute-done | bytes 2097184 | tf_op jit(solution)/shard_map/ppermute | solution.py:10
  42.4 3.8 %broadcast_select_fusion.1 = (bf16[2,1024,512]{2,1,0:T(8,128)(2,1)}, bf16[2,1024,512]{2,1,0:T(8,128)(2,1)}) fusion(bf16[2,1024,512]{2,1,0:T(8,128)(2,1)} %collective-permute-done, pred[]{:T(512)S(6)} %eq.36, bf16[1,2,1024,512]{3,2,1,0:T(8,128)(2,1)S(1)} %copy-done.1), kind=kLoop, calls=%fused_computation.27 | loop fusion | flops 2097152 | bytes 8388609 | tf_op jit(solution)/shard_map/jit(_where)/select_n | solution.py:33
  46.2 90.7 %all-to-all-done = bf16[2,128,8,1024]{3,2,0,1:T(8,128)(2,1)} async-done(((bf16[2,128,8,1024]{3,2,0,1:T(8,128)(2,1)}), bf16[2,128,8,1024]{3,2,0,1:T(8,128)(2,1)}, u32[]{:S(2)}, u32[]{:S(2)}) %all-to-all-start) | async-done | bytes 4194336 | tf_op jit(solution)/shard_map/all_to_all | solution.py:68
  137.0 0.0 copy-start.2
  137.0 5.0 %fusion.31 = bf16[1,128,8,512]{3,2,0,1:T(8,128)(2,1)S(1)} fusion(bf16[2,1024,512]{2,1,0:T(8,128)(2,1)} %get-tuple-element.8, bf16[2,1024,512]{2,1,0:T(8,128)(2,1)} %get-tuple-element.7, bf16[1,2,1024,512]{3,2,1,0:T(8,128)(2,1)} %param.10, bf16[2,128,8,1024]{3,2,0,1:T(8,128)(2,1)} %all-to-all-done), kind=kOutput, calls=%fused_computation.37 | convolution fusion | flops 2152726528 | bytes 8388608 | tf_op jit(solution)/shard_map/dot_general | solution.py:50
  141.9 0.0 copy-done.2
  141.9 5.5 %fusion.28 = bf16[1,128,8,512]{3,2,0,1:T(8,128)(2,1)} fusion(bf16[2,1024,512]{2,1,0:T(8,128)(2,1)S(1)} %copy-done.2, bf16[2,1024,512]{2,1,0:T(8,128)(2,1)} %get-tuple-element.8, bf16[1,2,1024,512]{3,2,1,0:T(8,128)(2,1)} %param.10, bf16[2,128,8,1024]{3,2,0,1:T(8,128)(2,1)} %all-to-all-done), kind=kOutput, calls=%fused_computation.36 | convolution fusion | flops 2152726528 | bytes 8388608 | tf_op jit(solution)/shard_map/dot_general | solution.py:50
  147.4 2.7 pad_maximum_fusion.3
  150.1 6.7 %all-to-all-start.3 = ((bf16[2,128,8,512]{3,2,0,1:T(8,128)(2,1)}), bf16[2,128,8,512]{3,2,0,1:T(8,128)(2,1)S(1)}, u32[]{:S(2)}, u32[]{:S(2)}) async-start(bf16[2,128,8,512]{3,2,0,1:T(8,128)(2,1)} %pad_maximum_fusion.3), calls=%async_computation.3 | async-start | bytes 4194304 | tf_op jit(solution)/shard_map/all_to_all | solution.py:104
  156.8 4.6 %slice_bitcast_fusion.2 = (bf16[1024,1024]{0,1:T(8,128)(2,1)}, bf16[1024,1024]{1,0:T(8,128)(2,1)S(1)}, bf16[1024,1024]{1,0:T(8,128)(2,1)S(1)}, bf16[1024,1024]{0...) fusion(bf16[2,128,8,1024]{3,2,0,1:T(8,128)(2,1)} %all-to-all-done), kind=kLoop, calls=%fused_computation.78 | loop fusion | bytes 16777216 | tf_op jit(solution)/shard_map/dot_general | solution.py:44
  161.5 0.0 copy-start.5
  161.5 0.0 copy-start.3
  161.5 2.5 fusion.35
  164.0 0.0 copy-done.5
  164.0 0.0 copy-done.3
  164.0 2.5 fusion.34
  166.4 0.2 pad_maximum_fusion.1
  166.7 2.5 copy.42
  169.1 39.6 %all-to-all-done.3 = bf16[2,128,8,512]{3,2,0,1:T(8,128)(2,1)S(1)} async-done(((bf16[2,128,8,512]{3,2,0,1:T(8,128)(2,1)}), bf16[2,128,8,512]{3,2,0,1:T(8,128)(2,1)S(1)}, u32[]{:S(2)}, u32[]{:S(2)}) %all-to-all-start.3) | async-done | bytes 2097184 | tf_op jit(solution)/shard_map/all_to_all | solution.py:104
  208.8 7.7 %all-to-all-start.1 = ((bf16[2,128,8,512]{3,2,0,1:T(8,128)(2,1)}), bf16[2,128,8,512]{3,2,0,1:T(8,128)(2,1)}, u32[]{:S(2)}, u32[]{:S(2)}) async-start(bf16[2,128,8,512]{3,2,0,1:T(8,128)(2,1)} %copy.42), calls=%async_computation.1 | async-start | bytes 4194304 | tf_op jit(solution)/shard_map/all_to_all | solution.py:89
  216.5 3.9 %copy.44 = bf16[1024,1024]{1,0:T(8,128)(2,1)} copy(bf16[1024,1024]{0,1:T(8,128)(2,1)} %get-tuple-element.9) | data formatting | bytes 4194304 | tf_op jit(solution)/shard_map/dot_general | solution.py:44
  220.4 3.9 %copy.46 = bf16[1024,1024]{1,0:T(8,128)(2,1)} copy(bf16[1024,1024]{0,1:T(8,128)(2,1)} %get-tuple-element.12) | data formatting | bytes 4194304 | tf_op jit(solution)/shard_map/dot_general | solution.py:44
  224.4 0.0 copy-start
  224.4 0.0 copy-start.4
  224.4 4.4 %fusion.39 = bf16[1,128,8,512]{3,1,2,0:T(8,128)(2,1)S(1)} fusion(bf16[128,8,1024]{2,1,0:T(8,128)(2,1)} %bitcast.108, bf16[1024,1024]{1,0:T(8,128)(2,1)} %copy-done.5, s32[]{:T(128)S(6)} %select_n.34), kind=kOutput, calls=%fused_computation.41 | convolution fusion | flops 1074266112 | bytes 4194308 | tf_op jit(solution)/shard_map/dot_general | solution.py:44
  228.8 0.0 copy-done
  228.8 0.0 copy-done.4
  228.8 2.4 fusion.36
  231.2 0.2 pad_maximum_fusion.2
  231.5 2.5 copy.48
  233.9 32.1 %all-to-all-done.1 = bf16[2,128,8,512]{3,2,0,1:T(8,128)(2,1)} async-done(((bf16[2,128,8,512]{3,2,0,1:T(8,128)(2,1)}), bf16[2,128,8,512]{3,2,0,1:T(8,128)(2,1)}, u32[]{:S(2)}, u32[]{:S(2)}) %all-to-all-start.1) | async-done | bytes 2097184 | tf_op jit(solution)/shard_map/all_to_all | solution.py:89
  266.0 7.7 %all-to-all-start.2 = ((bf16[2,128,8,512]{3,2,0,1:T(8,128)(2,1)}), bf16[2,128,8,512]{3,2,0,1:T(8,128)(2,1)}, u32[]{:S(2)}, u32[]{:S(2)}) async-start(bf16[2,128,8,512]{3,2,0,1:T(8,128)(2,1)} %copy.48), calls=%async_computation.2 | async-start | bytes 4194304 | tf_op jit(solution)/shard_map/all_to_all | solution.py:96
  273.8 1.5 copy.52
  275.2 3.1 gather_fusion.3
  278.3 1.7 copy.43
  280.1 2.7 bitcast_convert_fusion.1
  282.7 2.8 gather_fusion.1
  285.6 36.0 %all-to-all-done.2 = bf16[2,128,8,512]{3,2,0,1:T(8,128)(2,1)} async-done(((bf16[2,128,8,512]{3,2,0,1:T(8,128)(2,1)}), bf16[2,128,8,512]{3,2,0,1:T(8,128)(2,1)}, u32[]{:S(2)}, u32[]{:S(2)}) %all-to-all-start.2) | async-done | bytes 2097184 | tf_op jit(solution)/shard_map/all_to_all | solution.py:96
  321.6 1.7 copy.49
  323.3 2.7 bitcast_convert_fusion
  326.0 2.8 gather_fusion.2
  328.8 0.0 copy-start.6
  328.8 2.9 add.57
  331.7 0.0 copy-done.6
  331.7 1.4 add.58
  (4 shorter events, 0.0 us)
Async XLA Ops:
  22.4 15.6 %copy-start.1 = (bf16[1,2,1024,512]{3,2,1,0:T(8,128)(2,1)S(1)}, bf16[1,2,1024,512]{3,2,1,0:T(8,128)(2,1)}, u32[]{:S(2)}) copy-start(bf16[1,2,1024,512]{3,2,1,0:T(8,128)(2,1)} %param.9) | copy-start | bytes 6291460
  22.4 114.6 %all-to-all-start = ((bf16[2,128,8,1024]{3,2,0,1:T(8,128)(2,1)}), bf16[2,128,8,1024]{3,2,0,1:T(8,128)(2,1)}, u32[]{:S(2)}, u32[]{:S(2)}) async-start(bf16[2,128,8,1024]{3,2,0,1:T(8,128)(2,1)} %copy.37), calls=%async_computation | async-start | bytes 8388608 | tf_op jit(solution)/shard_map/all_to_all | solution.py:68
  38.0 4.4 %collective-permute-start = (bf16[2,1024,512]{2,1,0:T(8,128)(2,1)S(1)}, bf16[2,1024,512]{2,1,0:T(8,128)(2,1)}, u32[]{:S(2)}, u32[]{:S(2)}) collective-permute-start(bf16[2,1024,512]{2,1,0:T(8,128)(2,1)S(1)} %bitcast.109), channel_id=1, source_target_pairs={{0,128},{128,0},{1,129},{129,1},{2,130},{130,2},{3,131},{131,3},{4... | collective-permute-start | bytes 6291464 | tf_op jit(solution)/shard_map/ppermute | solution.py:10
  137.0 5.0 %copy-start.2 = (bf16[2,1024,512]{2,1,0:T(8,128)(2,1)S(1)}, bf16[2,1024,512]{2,1,0:T(8,128)(2,1)}, u32[]{:S(2)}) copy-start(bf16[2,1024,512]{2,1,0:T(8,128)(2,1)} %get-tuple-element.7) | copy-start | bytes 6291460
  150.1 58.6 %all-to-all-start.3 = ((bf16[2,128,8,512]{3,2,0,1:T(8,128)(2,1)}), bf16[2,128,8,512]{3,2,0,1:T(8,128)(2,1)S(1)}, u32[]{:S(2)}, u32[]{:S(2)}) async-start(bf16[2,128,8,512]{3,2,0,1:T(8,128)(2,1)} %pad_maximum_fusion.3), calls=%async_computation.3 | async-start | bytes 4194304 | tf_op jit(solution)/shard_map/all_to_all | solution.py:104
  161.5 2.5 copy-start.5
  161.5 2.5 copy-start.3
  208.8 57.3 %all-to-all-start.1 = ((bf16[2,128,8,512]{3,2,0,1:T(8,128)(2,1)}), bf16[2,128,8,512]{3,2,0,1:T(8,128)(2,1)}, u32[]{:S(2)}, u32[]{:S(2)}) async-start(bf16[2,128,8,512]{3,2,0,1:T(8,128)(2,1)} %copy.42), calls=%async_computation.1 | async-start | bytes 4194304 | tf_op jit(solution)/shard_map/all_to_all | solution.py:89
  224.4 4.4 %copy-start = (bf16[1024,1024]{1,0:T(8,128)(2,1)S(1)}, bf16[1024,1024]{1,0:T(8,128)(2,1)}, u32[]{:S(2)}) copy-start(bf16[1024,1024]{1,0:T(8,128)(2,1)} %copy.46) | copy-start | bytes 6291460
  224.4 4.4 %copy-start.4 = (bf16[1024,1024]{1,0:T(8,128)(2,1)S(1)}, bf16[1024,1024]{1,0:T(8,128)(2,1)}, u32[]{:S(2)}) copy-start(bf16[1024,1024]{1,0:T(8,128)(2,1)} %copy-done.3) | copy-start | bytes 6291460
  266.0 55.5 %all-to-all-start.2 = ((bf16[2,128,8,512]{3,2,0,1:T(8,128)(2,1)}), bf16[2,128,8,512]{3,2,0,1:T(8,128)(2,1)}, u32[]{:S(2)}, u32[]{:S(2)}) async-start(bf16[2,128,8,512]{3,2,0,1:T(8,128)(2,1)} %copy.48), calls=%async_computation.2 | async-start | bytes 4194304 | tf_op jit(solution)/shard_map/all_to_all | solution.py:96
  328.8 2.9 copy-start.6
where the time goes:
time: 334 us; the launch traced here: 333 us
  waiting for transfers between devices  203 us (61%)
  local copies, waits for them, and re-layouts  38.8 us (12%)
  starting transfers between devices  37.8 us (11%)
  matrix products  22.2 us (7%)
  other arithmetic  19.1 us (6%)
  blocking collectives  11.6 us (3%)
    all_to_all x1, waiting for transfers between devices, per_device(): lax.all_to_all(outgoing, 'shard', split_axis=1, concat_axis=1, tiled=True)  90.7 us
    all_to_all x1, waiting for transfers between devices, per_device(): lax.all_to_all(jnp.stack(new_blocks).reshape(owner_shape), 'shard', split...  39.6 us
    all_to_all x1, waiting for transfers between devices, per_device(): lax.all_to_all(jnp.stack(gram_right).reshape(owner_shape).astype(jnp.bflo...  36 us
    all_to_all x1, waiting for transfers between devices, per_device(): lax.all_to_all(jnp.stack(gram_left).reshape(owner_shape).astype(jnp.bfloa...  32.1 us
    all_to_all x1, starting transfers between devices, per_device(): lax.all_to_all(outgoing, 'shard', split_axis=1, concat_axis=1, tiled=True)  15.6 us
    dot_general x3, local copies, waits for them, and re-layouts, block_work(): lax.dot_general(full_grad, grad_cols, (((0,), (0,)), ((), ())), preferred...  12.5 us
    psum x1, blocking collectives, per_device(): replica_total = lax.psum(gradients[0], 'rep')  11.6 us
    dot_general x2, matrix products, block_work(): jnp.dot(left_full, applied, preferred_element_type=jnp.float32)  10.4 us
  transfers between devices with their start and end apart: 5, of which 5 were waited for; matrix products, arithmetic and copies ran while one was open for 14% of the time, Pallas kernels for 0%

commit v1 on v0

v1 whole, which is shorter than its diff:
```python
from functools import partial

import jax
import jax.numpy as jnp
from jax import lax
from jax.experimental import pallas as pl
from jax.experimental.pallas import tpu as pltpu
from jax.sharding import PartitionSpec as P

DOUBLE = 32
SINGLE = 24
PIECES = 4
SMEM = pl.BlockSpec(memory_space=pltpu.SMEM)
ANY = pl.BlockSpec(memory_space=pl.ANY)
VMEM_BYTES = 56 * 1024 * 1024


def whole_gram_counts(blocks, owners):
    idle = owners - DOUBLE - SINGLE
    shared = SINGLE // 2
    return idle, idle + shared


def plan_kernel(owner_ref, send_ref, spot_ref, held_ref, rank_ref, idle_ref, single_ref):
    blocks = owner_ref.shape[0]
    owners = held_ref.shape[0]
    idle_blocks, split_from = whole_gram_counts(blocks, owners)
    pieces = 2 * PIECES * (blocks - split_from)

    def clear(o, carry):
        held_ref[o] = 0
        return carry

    lax.fori_loop(0, owners, clear, 0, unroll=8)

    def place(b, carry):
        o = owner_ref[b]
        slot = held_ref[o]
        send_ref[2 * o + slot] = b
        spot_ref[b] = 2 * o + slot
        held_ref[o] = slot + 1
        return carry

    lax.fori_loop(0, blocks, place, 0, unroll=4)

    def fill(o, carry):
        idles, singles = carry
        held = held_ref[o]
        is_idle = held == 0
        is_single = held == 1
        idle_ref[jnp.where(is_idle, idles, owners - 1)] = o
        single_ref[jnp.where(is_single, singles, owners - 1)] = o
        rank_ref[o] = jnp.where(is_idle, idles, singles)
        extra = jnp.where(idles < pieces, split_from + idles // (2 * PIECES), 0)
        send_ref[2 * o] = jnp.where(is_idle, idles, send_ref[2 * o])
        send_ref[2 * o + 1] = jnp.where(
            is_idle,
            extra,
            jnp.where(is_single, idle_blocks + singles // 2, send_ref[2 * o + 1]),
        )
        return (idles + is_idle.astype(jnp.int32), singles + is_single.astype(jnp.int32))

    lax.fori_loop(0, owners, fill, (jnp.int32(0), jnp.int32(0)), unroll=4)


def make_plan(block_owner, owners):
    blocks = block_owner.shape[0]
    sizes = (2 * owners, blocks, owners, owners, owners, owners)
    return pl.pallas_call(
        plan_kernel,
        out_shape=[jax.ShapeDtypeStruct((n,), jnp.int32) for n in sizes],
        in_specs=[SMEM],
        out_specs=[SMEM] * len(sizes),
        cost_estimate=pl.CostEstimate(flops=0, bytes_accessed=8192, transcendentals=0),
        name="plan",
    )(block_owner)


def dispatch_kernel(side_ref, send_ref, mine_ref, other_ref, out_ref):
    step = pl.program_id(0)
    dests = out_ref.shape[0]
    half = mine_ref.shape[-1]

    def one(i, carry):
        for slot in range(2):
            b = send_ref[2 * (step * dests + i) + slot]
            out_ref[i, :, slot * half : (slot + 1) * half] = (mine_ref[b] + other_ref[b]).astype(
                jnp.bfloat16
            )
        return carry

    lax.fori_loop(0, dests, one, 0, unroll=4)


def dispatch(side, send, gradient, other, owners):
    blocks, rows, width = gradient.shape
    half = width // 2
    steps = 4
    return pl.pallas_call(
        dispatch_kernel,
        grid_spec=pltpu.PrefetchScalarGridSpec(
            num_scalar_prefetch=2,
            grid=(steps,),
            in_specs=[
                pl.BlockSpec((blocks, rows, half), lambda i, side, send: (0, 0, side[0])),
                pl.BlockSpec((blocks, rows, half), lambda i, side, send: (0, 0, 0)),
            ],
            out_specs=pl.BlockSpec(
                (owners // steps, rows, width), lambda i, side, send: (i, 0, 0)
            ),
        ),
        out_shape=jax.ShapeDtypeStruct((owners, rows, width), jnp.bfloat16),
        compiler_params=pltpu.CompilerParams(vmem_limit_bytes=VMEM_BYTES),
        cost_estimate=pl.CostEstimate(flops=0, bytes_accessed=5 << 20, transcendentals=0),
        name="dispatch",
    )(side, send, gradient, other)


def jobs_kernel(
    me_ref,
    held_ref,
    rank_ref,
    own_ref,
    other_ref,
    left_own_ref,
    left_other_ref,
    right_ref,
    out_ref,
    grad,
    left,
    right,
    applied,
    sems,
):
    size = own_ref.shape[0]
    half = size // 2
    quarter = half // PIECES
    side = me_ref[0]
    me = me_ref[1]
    held = held_ref[me]
    rank = rank_ref[me]
    here = pl.multiple_of(side * half, half)
    there = pl.multiple_of(half - side * half, half)
    tile = 256

    def columns(start):
        return pl.ds(start, half)

    loads = []
    for slot in range(2):
        part = pl.ds(slot * half, half)
        loads.append(
            [
                (own_ref.at[:, part], grad.at[slot, :, columns(here)]),
                (other_ref.at[:, part], grad.at[slot, :, columns(there)]),
                (right_ref.at[slot], right.at[slot]),
                (left_own_ref.at[slot], left.at[slot, :, columns(here)]),
                (left_other_ref.at[slot], left.at[slot, :, columns(there)]),
            ]
        )
    copies = [
        [
            pltpu.make_async_copy(source, target, sems.at[slot, i])
            for i, (source, target) in enumerate(loads[slot])
        ]
        for slot in range(2)
    ]
    for slot in range(2):
        for copy in copies[slot]:
            copy.start()

    def tiles(body):
        def step(i, carry):
            body(pl.ds(pl.multiple_of(i * tile, tile), tile))
            return carry

        lax.fori_loop(0, size // tile, step, 0)

    def update(slot):
        target = pl.ds(slot * half, half)

        def first(rows):
            applied[rows, :] = jnp.dot(
                grad[slot, rows, :], right[slot], preferred_element_type=jnp.float32
            ).astype(jnp.bfloat16)

        def second(rows):
            out_ref[rows, target] = jnp.dot(
                left[slot, rows, :], applied[...], preferred_element_type=jnp.float32
            ).astype(jnp.bfloat16)

        tiles(first)
        copies[slot][3].wait()
        copies[slot][4].wait()
        tiles(second)

    def left_gram(slot, start, count, target):
        def body(rows):
            out_ref[rows, target] = lax.dot_general(
                grad[slot, rows, :],
                grad[slot, pl.ds(start, count), :],
                (((1,), (1,)), ((), ())),
                preferred_element_type=jnp.float32,
            ).astype(jnp.bfloat16)

        tiles(body)

    def right_gram(slot, start, count, target):
        def body(rows):
            out_ref[rows, target] = lax.dot_general(
                grad[slot, :, rows],
                grad[slot, :, pl.ds(start, count)],
                (((0,), (0,)), ((), ())),
                preferred_element_type=jnp.float32,
            ).astype(jnp.bfloat16)

        tiles(body)

    def skip_left(slot):
        copies[slot][3].wait()
        copies[slot][4].wait()

    first_part = pl.ds(0, half)
    second_part = pl.ds(half, half)
    last_part = pl.ds(size, quarter)

    for copy in copies[0][:3]:
        copy.wait()

    @pl.when(held > 0)
    def _():
        update(0)

    @pl.when(held == 0)
    def _():
        skip_left(0)
        left_gram(0, here, half, first_part)
        right_gram(0, here, half, second_part)

    for copy in copies[1][:3]:
        copy.wait()

    @pl.when(held == 2)
    def _():
        update(1)

    @pl.when(held < 2)
    def _():
        skip_left(1)

    @pl.when((held == 1) & (rank % 2 == 0))
    def _():
        left_gram(1, here, half, second_part)

    @pl.when((held == 1) & (rank % 2 == 1))
    def _():
        right_gram(1, here, half, second_part)

    piece = rank % (2 * PIECES)
    start = pl.multiple_of(here + (piece % PIECES) * quarter, quarter)

    @pl.when((held == 0) & (piece < PIECES))
    def _():
        left_gram(1, start, quarter, last_part)

    @pl.when((held == 0) & (piece >= PIECES))
    def _():
        right_gram(1, start, quarter, last_part)


def run_jobs(me, held, rank, own, other, left_own, left_other, right_own):
    size = own.shape[0]
    half = size // 2
    width = size + half // PIECES
    bf16 = jnp.bfloat16
    return pl.pallas_call(
        jobs_kernel,
        in_specs=[SMEM] * 3 + [ANY] * 5,
        out_specs=pl.BlockSpec(memory_space=pltpu.VMEM),
        out_shape=jax.ShapeDtypeStruct((size, width), bf16),
        scratch_shapes=[
            pltpu.VMEM((2, size, size), bf16),
            pltpu.VMEM((2, size, size), bf16),
            pltpu.VMEM((2, size, half), bf16),
            pltpu.VMEM((size, half), bf16),
            pltpu.SemaphoreType.DMA((2, 5)),
        ],
        compiler_params=pltpu.CompilerParams(vmem_limit_bytes=VMEM_BYTES),
        cost_estimate=pl.CostEstimate(
            flops=8 * size * size * half, bytes_accessed=12 << 20, transcendentals=0
        ),
        name="jobs",
    )(me, held, rank, own, other, left_own, left_other, right_own)


def finish_kernel(
    spot_ref, idle_ref, single_ref, back_ref, left_ref, right_ref, new_left, new_right, update
):
    step = pl.program_id(0)
    count, _, half = left_ref.shape
    owners = back_ref.shape[0]
    quarter = half // PIECES
    blocks = spot_ref.shape[0]
    idle_blocks, split_from = whole_gram_counts(blocks, owners)
    f32 = jnp.float32

    def part(source, slot):
        return back_ref[source, :, slot * half : (slot + 1) * half]

    def one(i, carry):
        b = step * count + i
        spot = spot_ref[b]
        column = pl.multiple_of((spot % 2) * half, half)
        update[i] = back_ref[spot // 2, :, pl.ds(column, half)]

        @pl.when(b < idle_blocks)
        def _():
            source = idle_ref[b]
            new_left[i] = left_ref[i] + part(source, 0).astype(f32)
            new_right[i] = right_ref[i] + part(source, 1).astype(f32)

        @pl.when((b >= idle_blocks) & (b < split_from))
        def _():
            at = 2 * (b - idle_blocks)
            new_left[i] = left_ref[i] + part(single_ref[at], 1).astype(f32)
            new_right[i] = right_ref[i] + part(single_ref[at + 1], 1).astype(f32)

        @pl.when(b >= split_from)
        def _():
            at = 2 * PIECES * (b - split_from)
            for k in range(PIECES):
                span = pl.ds(k * quarter, quarter)
                last = pl.ds(2 * half, quarter)
                new_left[i, :, span] = left_ref[i, :, span] + back_ref[
                    idle_ref[at + k], :, last
                ].astype(f32)
                new_right[i, :, span] = right_ref[i, :, span] + back_ref[
                    idle_ref[at + PIECES + k], :, last
                ].astype(f32)

        return carry

    lax.fori_loop(0, count, one, 0)


def finish(spot, idle, single, back, left_stats, right_stats):
    blocks, rows, half = left_stats.shape
    steps = 4
    piece = pl.BlockSpec((blocks // steps, rows, half), lambda i, *_: (i, 0, 0))
    whole = pl.BlockSpec(back.shape, lambda i, *_: (0, 0, 0))
    stats = jax.ShapeDtypeStruct(left_stats.shape, jnp.float32)
    return pl.pallas_call(
        finish_kernel,
        grid_spec=pltpu.PrefetchScalarGridSpec(
            num_scalar_prefetch=3,
            grid=(steps,),
            in_specs=[whole, piece, piece],
            out_specs=[piece, piece, piece],
        ),
        out_shape=[stats, stats, jax.ShapeDtypeStruct(left_stats.shape, jnp.bfloat16)],
        compiler_params=pltpu.CompilerParams(vmem_limit_bytes=VMEM_BYTES),
        cost_estimate=pl.CostEstimate(flops=0, bytes_accessed=9 << 20, transcendentals=0),
        name="finish",
    )(spot, idle, single, back, left_stats, right_stats)


def per_device(gradients, left_stats, right_stats, left_root, right_root, block_owner):
    owners = lax.axis_size("shard")
    blocks, rows, half = left_stats.shape
    size = 2 * half
    side = lax.axis_index("rep")
    swapped = partial(lax.ppermute, axis_name="rep", perm=[(0, 1), (1, 0)])
    me = jnp.stack([side, lax.axis_index("shard")]).astype(jnp.int32)
    gradient = gradients[0]
    away = lax.dynamic_slice_in_dim(gradient, half - side * half, half, 2)
    other_gradient = swapped(away)
    send, spot, held, rank, idle, single = make_plan(block_owner, owners)
    outgoing = dispatch(me[:1], send, gradient, other_gradient, owners)
    other_left = swapped(left_root[0])
    arrived = lax.all_to_all(outgoing, "shard", split_axis=0, concat_axis=0, tiled=True)
    own = arrived.reshape(size, size)
    other = swapped(own)
    results = run_jobs(me, held, rank, own, other, left_root[0], other_left, right_root[0])
    back = lax.all_to_all(
        results.reshape(owners, rows, -1), "shard", split_axis=0, concat_axis=0, tiled=True
    )
    return tuple(finish(spot, idle, single, back, left_stats, right_stats))


def solution(mesh):
    return jax.shard_map(
        per_device,
        mesh=mesh,
        in_specs=(
            P("rep", None, "shard", None),
            P(None, "shard", "rep"),
            P(None, "shard", "rep"),
            P("shard", None, None, "rep"),
            P("shard", None, None, "rep"),
            P(),
        ),
        out_specs=(P(None, "shard", "rep"), P(None, "shard", "rep"), P(None, "shard", "rep")),
        check_vma=False,
    )
```

time: 334 us -> 172 us (0.51)
  waiting for transfers between devices: 203 us -> 58 us
  blocking collectives: 11.6 us -> 67.8 us
  local copies, waits for them, and re-layouts: 38.8 us -> 2.57 us
  Pallas kernels: 0 us -> 26.1 us
  starting transfers between devices: 37.8 us -> 15.2 us
  matrix products: 22.2 us -> 0 us
  other arithmetic: 19.1 us -> 0.67 us
    all_to_all x4 -> x1, waiting for transfers between devices: 198 us -> 54.4 us  [per_device(): lax.all_to_all(outgoing, 'shard', split_axis=0, concat_axis=0, tiled=True)]
    all_to_all x0 -> x1, blocking collectives: none -> 67.8 us  [per_device(): lax.all_to_all(results.reshape(owners, rows, -1), 'shard', split_axis=0,...]
    pallas_call x0 -> x4, Pallas kernels: none -> 26.1 us  [the longest x1 9.72 us: run_jobs(): pl.pallas_call(jobs_kernel, in_specs=[SMEM] * 3 + [ANY] * 5, out_specs=pl...]
    all_to_all x4 -> x1, starting transfers between devices: 37.7 us -> 15 us  [per_device(): lax.all_to_all(outgoing, 'shard', split_axis=0, concat_axis=0, tiled=True)]
    dot_general x6 -> x0, matrix products: 22.2 us -> none  [the longest x2 10.4 us: block_work(): jnp.dot(left_full, applied, preferred_element_type=jnp.float32)]
    dot_general x3 -> x0, local copies, waits for them, and re-layouts: 12.5 us -> none  [block_work(): lax.dot_general(full_grad, grad_cols, (((0,), (0,)), ((), ())), preferred...]
    psum x1 -> x0, blocking collectives: 11.6 us -> none  [per_device(): replica_total = lax.psum(gradients[0], 'rep')]
    gather x4 -> x0, local copies, waits for them, and re-layouts: 11.5 us -> none  [the longest x1 3.08 us: per_device(): update = update_back.reshape(flat_shape)[table_pos]]
  transfers between devices with their start and end apart: 5 -> 4, of which waited for: 5 -> 2; matrix products, arithmetic and copies ran while one was open for 14% -> 0% of each run, Pallas kernels for 0% -> 3%
where the time goes in v1:
time: 172 us; the launch traced here: 171 us
  blocking collectives  67.8 us (39%)
  waiting for transfers between devices  58 us (34%)
  Pallas kernels  26.1 us (15%)
  starting transfers between devices  15.2 us (9%)
  local copies, waits for them, and re-layouts  2.57 us (1%)
    all_to_all x1, blocking collectives, per_device(): lax.all_to_all(results.reshape(owners, rows, -1), 'shard', split_axis=0,...  67.8 us
    all_to_all x1, waiting for transfers between devices, per_device(): lax.all_to_all(outgoing, 'shard', split_axis=0, concat_axis=0, tiled=True)  54.4 us
    all_to_all x1, starting transfers between devices, per_device(): lax.all_to_all(outgoing, 'shard', split_axis=0, concat_axis=0, tiled=True)  15 us
    pallas_call x1, Pallas kernels, run_jobs(): pl.pallas_call(jobs_kernel, in_specs=[SMEM] * 3 + [ANY] * 5, out_specs=pl...  9.72 us
    pallas_call x1, Pallas kernels, finish(): pl.pallas_call(finish_kernel, grid_spec=pltpu.PrefetchScalarGridSpec(num_...  7.34 us
    pallas_call x1, Pallas kernels, dispatch(): pl.pallas_call(dispatch_kernel, grid_spec=pltpu.PrefetchScalarGridSpec(nu...  4.65 us
    pallas_call x1, Pallas kernels, make_plan(): pl.pallas_call(plan_kernel, out_shape=[jax.ShapeDtypeStruct((n,), jnp.int...  4.39 us
    ppermute x1, waiting for transfers between devices, per_device(): other = swapped(own)  3.61 us
  transfers between devices with their start and end apart: 4, of which 2 were waited for; matrix products, arithmetic and copies ran while one was open for 0% of the time, Pallas kernels for 3%

profile of v1, /device:TPU:32, one launch (start us, length us, event | category | flops | bytes accessed | tf_op | source)
XLA Modules:
  0.0 171.0 jit_solution(6065753454680222455)
XLA Ops:
  0.6 1.5 dynamic-slice_bitcast_fusion
  2.1 0.1 collective-permute-start
  2.2 4.4 %plan.1 = (s32[256]{0:T(256)}, s32[88]{0:T(128)}, s32[128]{0:T(128)}, s32[128]{0:T(128)}, s32[128]{0:T(128)}, /*index=5*/s32[128]{0:T(128)}) custom-call(s32[88]{0:T(128)} %owner_ref.1), custom_call_target="tpu_custom_call" | custom-call | bytes 8192 | tf_op jit(solution)/shard_map/plan/pallas_call | solution.py:69
  6.6 0.0 collective-permute-done.other_ref
  6.6 0.0 copy-start.1
  6.6 1.1 copy-done.1
  7.7 4.6 %dispatch.1 = bf16[128,8,1024]{2,1,0:T(8,128)(2,1)} custom-call(s32[1]{0:T(128)} %bitcast.side_ref, s32[256]{0:T(256)} %get-tuple-element.14.send_ref, f32[88,8,1024]{2,1,0:T(8,128)} %bitcast.9, f32[88,8,512]{2,1,0:T(8,128)} %copy-done.1), custom_call_target="tpu_custom_call" | custom-call | bytes 5242880 | tf_op jit(solution)/shard_map/dispatch/pallas_call | solution.py:99
  12.4 15.0 %all-to-all-start = ((bf16[128,8,1024]{2,1,0:T(8,128)(2,1)}), bf16[128,8,1024]{2,1,0:T(8,128)(2,1)S(1)}, u32[]{:S(2)}, u32[]{:S(2)}) async-start(bf16[128,8,1024]{2,1,0:T(8,128)(2,1)} %dispatch.1), calls=%async_computation | async-start | bytes 4194304 | tf_op jit(solution)/shard_map/all_to_all | solution.py:380
  27.4 0.1 collective-permute-start.2
  27.5 54.4 %all-to-all-done = bf16[128,8,1024]{2,1,0:T(8,128)(2,1)S(1)} async-done(((bf16[128,8,1024]{2,1,0:T(8,128)(2,1)}), bf16[128,8,1024]{2,1,0:T(8,128)(2,1)S(1)}, u32[]{:S(2)}, u32[]{:S(2)}) %all-to-all-start) | async-done | bytes 2097184 | tf_op jit(solution)/shard_map/all_to_all | solution.py:380
  81.9 0.0 copy-start
  81.9 0.0 collective-permute-start.1
  81.9 0.7 pad_add_fusion.me_ref
  82.5 0.0 collective-permute-done.2.left_other_ref
  82.5 3.6 %collective-permute-done.1.other_ref = bf16[1024,1024]{1,0:T(8,128)(2,1)} collective-permute-done((bf16[1024,1024]{1,0:T(8,128)(2,1)S(1)}, bf16[1024,1024]{1,0:T(8,128)(2,1)}, u32[]{:S(2)}, u32[]{:S(2)}) %collective-permute-start.1) | collective-permute-done | bytes 2097184 | tf_op jit(solution)/shard_map/ppermute | solution.py:382
  86.2 0.0 copy-done
  86.2 9.7 %jobs.1 = bf16[1024,1152]{1,0:T(8,128)(2,1)} custom-call(s32[2]{0:T(128)} %pad_add_fusion.me_ref, s32[128]{0:T(128)} %get-tuple-element.12.held_ref, s32[128]{0:T(128)} %get-tuple-element.13.rank_ref, bf16[1024,1024]{1,0:T(8,128)(2,1)} %bitcast.12, bf16[1024,1024]{1,0:T(8,128)(2,1)} %collective-permute-done.1.other_ref, bf16[2,1024,512]{2,1,0:T(8,128)(2,1)} %bitcast.14, ...), custom_call_target="tpu_custom_call" | custom-call | flops 4294967296 | bytes 12582912 | tf_op jit(solution)/shard_map/jobs/pallas_call | solution.py:276
  95.9 67.8 %all_to_all.10.back_ref = bf16[128,8,1152]{2,1,0:T(8,128)(2,1)} all-to-all(bf16[128,8,1152]{2,1,0:T(8,128)(2,1)} %bitcast.10), channel_id=1, replica_groups=mesh['rep'=2,'shard'=128] {'shard'}, dimensions={0} | all-to-all | bytes 4718592 | tf_op jit(solution)/shard_map/all_to_all | solution.py:384
  163.7 7.3 %finish.1 = (f32[88,8,512]{2,1,0:T(8,128)}, f32[88,8,512]{2,1,0:T(8,128)}, bf16[88,8,512]{2,1,0:T(8,128)(2,1)}) custom-call(s32[88]{0:T(128)} %get-tuple-element.9.spot_ref, s32[128]{0:T(128)} %get-tuple-element.10.idle_ref, s32[128]{0:T(128)} %get-tuple-element.11.single_ref, bf16[128,8,1152]{2,1,0:T(8,128)(2,1)} %all_to_all.10.back_ref, ...), custom_call_target="tpu_custom_call" | custom-call | bytes 9437184 | tf_op jit(solution)/shard_map/finish/pallas_call | solution.py:352
Async XLA Ops:
  2.1 4.5 %collective-permute-start = (f32[88,8,512]{2,1,0:T(8,128)S(1)}, f32[88,8,512]{2,1,0:T(8,128)S(1)}, u32[]{:S(2)}, u32[]{:S(2)}) collective-permute-start(f32[88,8,512]{2,1,0:T(8,128)S(1)} %dynamic-slice_bitcast_fusion), channel_id=1, source_target_pairs={{0,128},{128,0},{1,129},{129,1},{2,130},{130,2},{3,131},{131,3},{4... | collective-permute-start | bytes 4325384 | tf_op jit(solution)/shard_map/ppermute | solution.py:376
  6.6 1.1 copy-start.1
  12.4 69.5 %all-to-all-start = ((bf16[128,8,1024]{2,1,0:T(8,128)(2,1)}), bf16[128,8,1024]{2,1,0:T(8,128)(2,1)S(1)}, u32[]{:S(2)}, u32[]{:S(2)}) async-start(bf16[128,8,1024]{2,1,0:T(8,128)(2,1)} %dispatch.1), calls=%async_computation | async-start | bytes 4194304 | tf_op jit(solution)/shard_map/all_to_all | solution.py:380
  27.4 55.2 %collective-permute-start.2 = (bf16[2,1024,512]{2,1,0:T(8,128)(2,1)}, bf16[2,1024,512]{2,1,0:T(8,128)(2,1)}, u32[]{:S(2)}, u32[]{:S(2)}) collective-permute-start(bf16[2,1024,512]{2,1,0:T(8,128)(2,1)} %bitcast.13), channel_id=1, source_target_pairs={{0,128},{128,0},{1,129},{129,1},{2,130},{130,2},{3,131},{131,3},{4... | collective-permute-start | bytes 6291464 | tf_op jit(solution)/shard_map/ppermute | solution.py:379
  81.9 4.3 %copy-start = (bf16[128,8,1024]{2,1,0:T(8,128)(2,1)}, bf16[128,8,1024]{2,1,0:T(8,128)(2,1)S(1)}, u32[]{:S(2)}) copy-start(bf16[128,8,1024]{2,1,0:T(8,128)(2,1)S(1)} %all-to-all-done) | copy-start | bytes 6291460
  81.9 4.3 %collective-permute-start.1 = (bf16[1024,1024]{1,0:T(8,128)(2,1)S(1)}, bf16[1024,1024]{1,0:T(8,128)(2,1)}, u32[]{:S(2)}, u32[]{:S(2)}) collective-permute-start(bf16[1024,1024]{1,0:T(8,128)(2,1)S(1)} %bitcast.11), channel_id=1, source_target_pairs={{0,128},{128,0},{1,129},{129,1},{2,130},{130,2},{3,131},{131,3},{4... | collective-permute-start | bytes 6291464 | tf_op jit(solution)/shard_map/ppermute | solution.py:382

commit v2 on v1

v2 whole, which is shorter than its diff:
```python
from functools import partial

import jax
import jax.numpy as jnp
from jax import lax
from jax.experimental import pallas as pl
from jax.experimental.pallas import tpu as pltpu
from jax.sharding import PartitionSpec as P

DOUBLE = 32
SINGLE = 24
PIECES = 4
SMEM = pl.BlockSpec(memory_space=pltpu.SMEM)
WHOLE = pl.BlockSpec(memory_space=pltpu.VMEM)
ANY = pl.BlockSpec(memory_space=pl.ANY)
MIB = 1024 * 1024


def in_hbm(value):
    return pltpu.with_memory_space_constraint(value, pltpu.HBM)


def in_vmem(value):
    return pltpu.with_memory_space_constraint(value, pltpu.VMEM)


def whole_gram_counts(blocks, owners):
    idle = owners - DOUBLE - SINGLE
    shared = SINGLE // 2
    return idle, idle + shared


def plan_kernel(
    owner_ref,
    gradient_ref,
    send_ref,
    spot_ref,
    idle_ref,
    single_ref,
    job_ref,
    mine_ref,
    held_ref,
    sem,
):
    blocks = owner_ref.shape[0]
    owners = held_ref.shape[0]
    half = mine_ref.shape[-1]
    side = lax.axis_index("rep")
    me = lax.axis_index("shard")
    here = pl.ds(pl.multiple_of(side * half, half), half)
    copy = pltpu.make_async_copy(gradient_ref.at[:, :, here], mine_ref, sem)
    copy.start()
    idle_blocks, split_from = whole_gram_counts(blocks, owners)
    pieces = 2 * PIECES * (blocks - split_from)

    def clear(o, carry):
        held_ref[o] = 0
        return carry

    lax.fori_loop(0, owners, clear, 0, unroll=8)

    def place(b, carry):
        o = owner_ref[b]
        slot = held_ref[o]
        send_ref[2 * o + slot] = b
        spot_ref[b] = 2 * o + slot
        held_ref[o] = slot + 1
        return carry

    lax.fori_loop(0, blocks, place, 0, unroll=4)

    def fill(o, carry):
        idles, singles, rank = carry
        held = held_ref[o]
        is_idle = held == 0
        is_single = held == 1
        idle_ref[jnp.where(is_idle, idles, owners - 1)] = o
        single_ref[jnp.where(is_single, singles, owners - 1)] = o
        extra = jnp.where(idles < pieces, split_from + idles // (2 * PIECES), 0)
        send_ref[2 * o] = jnp.where(is_idle, idles, send_ref[2 * o])
        send_ref[2 * o + 1] = jnp.where(
            is_idle,
            extra,
            jnp.where(is_single, idle_blocks + singles // 2, send_ref[2 * o + 1]),
        )
        mine = jnp.where(is_idle, idles, singles)
        return (
            idles + is_idle.astype(jnp.int32),
            singles + is_single.astype(jnp.int32),
            jnp.where(o == me, mine, rank),
        )

    zero = jnp.int32(0)
    job_ref[0] = side
    job_ref[1] = held_ref[me]
    job_ref[2] = lax.fori_loop(0, owners, fill, (zero, zero, zero), unroll=4)[2]
    copy.wait()


def make_plan(block_owner, gradient, owners):
    blocks, rows, width = gradient.shape
    sizes = (2 * owners, blocks, owners, owners, 3)
    *tables, mine = pl.pallas_call(
        plan_kernel,
        out_shape=[jax.ShapeDtypeStruct((n,), jnp.int32) for n in sizes]
        + [jax.ShapeDtypeStruct((blocks, rows, width // 2), jnp.float32)],
        in_specs=[SMEM, ANY],
        out_specs=[SMEM] * len(sizes) + [WHOLE],
        scratch_shapes=[pltpu.SMEM((owners,), jnp.int32), pltpu.SemaphoreType.DMA],
        compiler_params=pltpu.CompilerParams(vmem_limit_bytes=4 * MIB),
        cost_estimate=pl.CostEstimate(flops=0, bytes_accessed=4 << 20, transcendentals=0),
        name="plan",
    )(in_hbm(block_owner), in_hbm(gradient))
    return tables + [mine]


def dispatch_kernel(job_ref, send_ref, mine_ref, other_ref, out_ref):
    dests, _, width = out_ref.shape
    half = width // 2
    here = pl.ds(pl.multiple_of(job_ref[0] * half, half), half)

    def one(dest, carry):
        for slot in range(2):
            b = send_ref[2 * dest + slot]
            out_ref[dest, :, slot * half : (slot + 1) * half] = (
                mine_ref[b] + other_ref[b, :, here]
            ).astype(jnp.bfloat16)
        return carry

    lax.fori_loop(0, dests, one, 0, unroll=4)


def dispatch(job, send, mine, other, owners):
    _, rows, width = other.shape
    return pl.pallas_call(
        dispatch_kernel,
        in_specs=[SMEM, SMEM, WHOLE, WHOLE],
        out_specs=WHOLE,
        out_shape=jax.ShapeDtypeStruct((owners, rows, width), jnp.bfloat16),
        compiler_params=pltpu.CompilerParams(vmem_limit_bytes=16 * MIB),
        cost_estimate=pl.CostEstimate(flops=0, bytes_accessed=5 << 20, transcendentals=0),
        name="dispatch",
    )(job, send, in_vmem(mine), other)


def fetch_kernel(*refs):
    count = len(refs) // 2
    sems = refs[-1]
    copies = [pltpu.make_async_copy(refs[i], refs[count + i], sems.at[i]) for i in range(count)]
    for copy in copies:
        copy.start()
    for copy in copies:
        copy.wait()


def fetch(*values):
    size = sum(value.size * value.dtype.itemsize for value in values)
    fetched = pl.pallas_call(
        fetch_kernel,
        in_specs=[ANY] * len(values),
        out_specs=[WHOLE] * len(values),
        out_shape=[jax.ShapeDtypeStruct(value.shape, value.dtype) for value in values],
        scratch_shapes=[pltpu.SemaphoreType.DMA((len(values),))],
        compiler_params=pltpu.CompilerParams(vmem_limit_bytes=16 * MIB),
        cost_estimate=pl.CostEstimate(flops=0, bytes_accessed=2 * size, transcendentals=0),
        name="fetch",
    )(*[in_hbm(value) for value in values])
    return [in_vmem(value) for value in fetched]


def jobs_kernel(
    job_ref, own_ref, other_ref, left_own, left_other, right, out_ref, applied
):
    size, width = own_ref.shape
    half = width // 2
    quarter = half // PIECES
    side = job_ref[0]
    held = job_ref[1]
    rank = job_ref[2]
    here = pl.multiple_of(side * half, half)
    there = pl.multiple_of(half - side * half, half)
    tile = 512

    def tiles(count, body):
        for at in range(0, count, tile):
            body(at)

    def rows_at(start):
        return pl.ds(pl.multiple_of(start, tile), tile)

    def product(a, b, dims):
        return lax.dot_general(
            a, b, ((dims[:1], dims[1:]), ((), ())), preferred_element_type=jnp.float32
        )

    def update(slot):
        span = pl.ds(slot * half, half)

        def first(at):
            rows = rows_at(at)
            total = product(own_ref[rows, span], right[slot, pl.ds(here, half), :], (1, 0))
            total += product(other_ref[rows, span], right[slot, pl.ds(there, half), :], (1, 0))
            applied[rows, :] = total.astype(jnp.bfloat16)

        def second(at):
            rows = rows_at(at)
            total = product(left_own[slot, rows, :], applied[pl.ds(here, half), :], (1, 0))
            total += product(left_other[slot, rows, :], applied[pl.ds(there, half), :], (1, 0))
            out_ref[rows, span] = total.astype(jnp.bfloat16)

        tiles(size, first)
        tiles(size, second)

    def left_gram(slot, start, count, target):
        span = pl.ds(slot * half, half)
        wanted = pl.ds(pl.multiple_of(here + start, quarter), count)

        def body(at):
            rows = rows_at(at)
            total = product(own_ref[rows, span], own_ref[wanted, span], (1, 1))
            total += product(other_ref[rows, span], other_ref[wanted, span], (1, 1))
            out_ref[rows, target] = total.astype(jnp.bfloat16)

        tiles(size, body)

    def right_gram(slot, start, count, target):
        wanted = pl.ds(pl.multiple_of(slot * half + start, quarter), count)
        for source, offset in ((own_ref, here), (other_ref, there)):

            def body(at):
                span = pl.ds(pl.multiple_of(slot * half + at, tile), tile)
                total = product(source[:, span], own_ref[:, wanted], (0, 0))
                out_ref[rows_at(offset + at), target] = total.astype(jnp.bfloat16)

            tiles(half, body)

    first_part = pl.ds(0, half)
    second_part = pl.ds(half, half)
    last_part = pl.ds(width, quarter)

    @pl.when(held > 0)
    def _():
        update(0)

    @pl.when(held == 0)
    def _():
        left_gram(0, 0, half, first_part)
        right_gram(0, 0, half, second_part)

    @pl.when(held == 2)
    def _():
        update(1)

    @pl.when((held == 1) & (rank % 2 == 0))
    def _():
        left_gram(1, 0, half, second_part)

    @pl.when((held == 1) & (rank % 2 == 1))
    def _():
        right_gram(1, 0, half, second_part)

    piece = rank % (2 * PIECES)
    start = (piece % PIECES) * quarter

    @pl.when((held == 0) & (piece < PIECES))
    def _():
        left_gram(1, start, quarter, last_part)

    @pl.when((held == 0) & (piece >= PIECES))
    def _():
        right_gram(1, start, quarter, last_part)


def run_jobs(job, own, other, left_own, left_other, right_own):
    size = own.shape[0]
    half = size // 2
    width = size + half // PIECES
    bf16 = jnp.bfloat16
    return pl.pallas_call(
        jobs_kernel,
        in_specs=[SMEM] + [WHOLE] * 5,
        out_specs=WHOLE,
        out_shape=jax.ShapeDtypeStruct((size, width), bf16),
        scratch_shapes=[pltpu.VMEM((size, half), bf16)],
        compiler_params=pltpu.CompilerParams(vmem_limit_bytes=20 * MIB),
        cost_estimate=pl.CostEstimate(
            flops=8 * size * size * half, bytes_accessed=12 << 20, transcendentals=0
        ),
        name="jobs",
    )(job, own, other, left_own, left_other, right_own)


def finish_kernel(
    spot_ref,
    idle_ref,
    single_ref,
    back_ref,
    left_ref,
    right_ref,
    left_out,
    right_out,
    update_out,
    new_left,
    new_right,
    update,
    sems,
):
    blocks, _, half = left_ref.shape
    owners = back_ref.shape[0]
    quarter = half // PIECES
    idle_blocks, split_from = whole_gram_counts(blocks, owners)
    f32 = jnp.float32

    def part(source, slot):
        return back_ref[source, :, slot * half : (slot + 1) * half].astype(f32)

    def applied(b):
        spot = spot_ref[b]
        column = pl.multiple_of((spot % 2) * half, half)
        update[b] = back_ref[spot // 2, :, pl.ds(column, half)]

    def whole_pair(b, carry):
        applied(b)
        source = idle_ref[b]
        new_left[b] = left_ref[b] + part(source, 0)
        new_right[b] = right_ref[b] + part(source, 1)
        return carry

    def shared_pair(b, carry):
        applied(b)
        at = 2 * (b - idle_blocks)
        new_left[b] = left_ref[b] + part(single_ref[at], 1)
        new_right[b] = right_ref[b] + part(single_ref[at + 1], 1)
        return carry

    def split_pair(b, carry):
        applied(b)
        at = 2 * PIECES * (b - split_from)
        last = pl.ds(2 * half, quarter)
        for k in range(PIECES):
            span = pl.ds(k * quarter, quarter)
            for new, old, source in (
                (new_left, left_ref, idle_ref[at + k]),
                (new_right, right_ref, idle_ref[at + PIECES + k]),
            ):
                new[b, :, span] = old[b, :, span] + back_ref[source, :, last].astype(f32)
        return carry

    copies = []

    def send(first, last):
        span = pl.ds(first, last - first)
        for source, target in ((new_left, left_out), (new_right, right_out), (update, update_out)):
            copy = pltpu.make_async_copy(source.at[span], target.at[span], sems.at[len(copies)])
            copy.start()
            copies.append(copy)

    third = idle_blocks // 3
    for first in range(0, idle_blocks, third):
        lax.fori_loop(first, first + third, whole_pair, 0, unroll=2)
        send(first, first + third)
    lax.fori_loop(idle_blocks, split_from, shared_pair, 0, unroll=2)
    lax.fori_loop(split_from, blocks, split_pair, 0)
    send(idle_blocks, blocks)
    for copy in copies:
        copy.wait()


def finish(spot, idle, single, back, left_stats, right_stats):
    shape = left_stats.shape
    kinds = (jnp.float32, jnp.float32, jnp.bfloat16)
    return pl.pallas_call(
        finish_kernel,
        in_specs=[SMEM] * 3 + [WHOLE] * 3,
        out_specs=[ANY] * 3,
        out_shape=[jax.ShapeDtypeStruct(shape, kind) for kind in kinds],
        scratch_shapes=[pltpu.VMEM(shape, kind) for kind in kinds]
        + [pltpu.SemaphoreType.DMA((12,))],
        compiler_params=pltpu.CompilerParams(vmem_limit_bytes=16 * MIB),
        cost_estimate=pl.CostEstimate(flops=0, bytes_accessed=9 << 20, transcendentals=0),
        name="finish",
    )(spot, idle, single, back, left_stats, right_stats)


def per_device(gradients, left_stats, right_stats, left_root, right_root, block_owner):
    owners = lax.axis_size("shard")
    blocks, rows, half = left_stats.shape
    size = 2 * half
    swapped = partial(lax.ppermute, axis_name="rep", perm=[(0, 1), (1, 0)])
    gradient = gradients[0]
    other_gradient = swapped(gradient)
    send, spot, idle, single, job, mine = make_plan(block_owner, gradient, owners)
    outgoing = dispatch(job, send, mine, other_gradient, owners)
    other_left = swapped(left_root[0])
    arrived = lax.all_to_all(outgoing, "shard", split_axis=0, concat_axis=0, tiled=True)
    own = arrived.reshape(size, size)
    other = swapped(own)
    roots = fetch(left_root[0], other_left, right_root[0])
    results = run_jobs(job, own, other, *roots)
    back = lax.all_to_all(
        results.reshape(owners, rows, -1), "shard", split_axis=0, concat_axis=0, tiled=True
    )
    return tuple(finish(spot, idle, single, back, left_stats, right_stats))


def solution(mesh):
    return jax.shard_map(
        per_device,
        mesh=mesh,
        in_specs=(
            P("rep", None, "shard", None),
            P(None, "shard", "rep"),
            P(None, "shard", "rep"),
            P("shard", None, None, "rep"),
            P("shard", None, None, "rep"),
            P(),
        ),
        out_specs=(P(None, "shard", "rep"), P(None, "shard", "rep"), P(None, "shard", "rep")),
        check_vma=False,
    )
```

time: 172 us -> 156 us (0.907)
  Pallas kernels: 26.1 us -> 16.5 us
  local copies, waits for them, and re-layouts: 2.57 us -> 0.01 us
  waiting for transfers between devices: 58 us -> 56.2 us
    pallas_call x3 -> x4, Pallas kernels: 21.7 us -> 11.9 us  [the longest x1 3.65 us: run_jobs(): pl.pallas_call(jobs_kernel, in_specs=[SMEM] + [WHOLE] * 5, out_specs=WHOL...]
    ppermute x1, waiting for transfers between devices: 3.61 us -> 1.26 us  [per_device(): other = swapped(own)]
  transfers between devices with their start and end apart: 4 -> 4, of which waited for: 2 -> 3; matrix products, arithmetic and copies ran while one was open for 0% -> 0% of each run, Pallas kernels for 3% -> 5%
where the time goes in v2:
time: 156 us
  blocking collectives  67.3 us (43%)
  waiting for transfers between devices  56.2 us (36%)
  Pallas kernels  16.5 us (11%)
  starting transfers between devices  15.2 us (10%)
    all_to_all x1, blocking collectives, per_device(): lax.all_to_all(results.reshape(owners, rows, -1), 'shard', split_axis=0,...  67.3 us
    all_to_all x1, waiting for transfers between devices, per_device(): lax.all_to_all(outgoing, 'shard', split_axis=0, concat_axis=0, tiled=True)  54 us
    all_to_all x1, starting transfers between devices, per_device(): lax.all_to_all(outgoing, 'shard', split_axis=0, concat_axis=0, tiled=True)  15 us
    pallas_call x1, Pallas kernels, make_plan(): pl.pallas_call(plan_kernel, out_shape=[jax.ShapeDtypeStruct((n,), jnp.int...  4.54 us
    pallas_call x1, Pallas kernels, run_jobs(): pl.pallas_call(jobs_kernel, in_specs=[SMEM] + [WHOLE] * 5, out_specs=WHOL...  3.65 us
  transfers between devices with their start and end apart: 4, of which 3 were waited for; matrix products, arithmetic and copies ran while one was open for 0% of the time, Pallas kernels for 5%

profile of v2, /device:TPU:32, one launch (start us, length us, event | category | flops | bytes accessed | tf_op | source)
XLA Modules:
  0.0 155.9 jit_solution(2248820575379642753)
XLA Ops:
  0.6 0.1 collective-permute-start
  0.7 4.5 %plan.1 = (s32[256]{0:T(256)S(1)}, s32[88]{0:T(128)S(1)}, s32[128]{0:T(128)S(1)}, s32[128]{0:T(128)S(1)}, s32[3]{0:T(128)S(1)}, /*index=5*/f32[88,8,512]{2,1,0:T(8,128)S(1)}) custom-call(s32[88]{0:T(128)} %owner_ref.1, f32[88,8,1024]{2,1,0:T(8,128)} %bitcast.9), custom_call_target="tpu_custom_call" | custom-call | bytes 4194304 | tf_op jit(solution)/shard_map/plan/pallas_call | solution.py:103
  5.3 0.9 collective-permute-done.other_ref
  6.2 2.7 %dispatch.1 = bf16[128,8,1024]{2,1,0:T(8,128)(2,1)} custom-call(s32[3]{0:T(128)S(1)} %get-tuple-element.15.job_ref, s32[256]{0:T(256)S(1)} %get-tuple-element.16.send_ref, f32[88,8,512]{2,1,0:T(8,128)S(1)} %get-tuple-element.17.mine_ref, f32[88,8,1024]{2,1,0:T(8,128)S(1)} %collective-permute-done.other_ref), custom_call_target="tpu_custom_call" | custom-call | bytes 5242880 | tf_op jit(solution)/shard_map/dispatch/pallas_call | solution.py:135
  8.9 15.0 %all-to-all-start = ((bf16[128,8,1024]{2,1,0:T(8,128)(2,1)}), bf16[128,8,1024]{2,1,0:T(8,128)(2,1)S(1)}, u32[]{:S(2)}, u32[]{:S(2)}) async-start(bf16[128,8,1024]{2,1,0:T(8,128)(2,1)} %dispatch.1), calls=%async_computation | async-start | bytes 4194304 | tf_op jit(solution)/shard_map/all_to_all | solution.py:395
  23.9 0.1 collective-permute-start.2
  24.0 54.0 %all-to-all-done = bf16[128,8,1024]{2,1,0:T(8,128)(2,1)S(1)} async-done(((bf16[128,8,1024]{2,1,0:T(8,128)(2,1)}), bf16[128,8,1024]{2,1,0:T(8,128)(2,1)S(1)}, u32[]{:S(2)}, u32[]{:S(2)}) %all-to-all-start) | async-done | bytes 2097184 | tf_op jit(solution)/shard_map/all_to_all | solution.py:395
  78.0 0.0 collective-permute-start.1
  78.0 0.0 collective-permute-done.2.refs_1_
  78.0 2.9 %fetch.1 = (bf16[2,1024,512]{2,1,0:T(8,128)(2,1)S(1)}, bf16[2,1024,512]{2,1,0:T(8,128)(2,1)S(1)}, bf16[2,1024,512]{2,1,0:T(8,128)(2,1)S(1)}) custom-call(bf16[2,1024,512]{2,1,0:T(8,128)(2,1)} %bitcast.11, bf16[2,1024,512]{2,1,0:T(8,128)(2,1)} %collective-permute-done.2.refs_1_, bf16[2,1024,512]{2,1,0:T(8,128)(2,1)} %bitcast.12), custom_call_target="tpu_custom_call" | custom-call | bytes 12582912 | tf_op jit(solution)/shard_map/fetch/pallas_call | solution.py:158
  80.9 1.3 collective-permute-done.1.other_ref
  82.2 3.7 %jobs.1 = bf16[1024,1152]{1,0:T(8,128)(2,1)S(1)} custom-call(s32[3]{0:T(128)S(1)} %get-tuple-element.15.job_ref, bf16[1024,1024]{1,0:T(8,128)(2,1)S(1)} %bitcast.7, bf16[1024,1024]{1,0:T(8,128)(2,1)S(1)} %collective-permute-done.1.other_ref, bf16[2,1024,512]{2,1,0:T(8,128)(2,1)S(1)} %get-tuple-element.18.left_own, ...), custom_call_target="tpu_custom_call" | custom-call | flops 4294967296 | bytes 12582912 | tf_op jit(solution)/shard_map/jobs/pallas_call | solution.py:279
  85.8 0.0 copy-start
  85.8 0.0 copy-start.1
  85.9 67.3 %all_to_all.10.back_ref = bf16[128,8,1152]{2,1,0:T(8,128)(2,1)S(1)} all-to-all(bf16[128,8,1152]{2,1,0:T(8,128)(2,1)S(1)} %bitcast.5), channel_id=1, replica_groups=mesh['rep'=2,'shard'=128] {'shard'}, dimensions={0} | all-to-all | bytes 4718592 | tf_op jit(solution)/shard_map/all_to_all | solution.py:400
  153.1 0.0 copy-done
  153.1 0.0 copy-done.1
  153.1 2.7 %finish.1 = (f32[88,8,512]{2,1,0:T(8,128)}, f32[88,8,512]{2,1,0:T(8,128)}, bf16[88,8,512]{2,1,0:T(8,128)(2,1)}) custom-call(s32[88]{0:T(128)S(1)} %get-tuple-element.12.spot_ref, s32[128]{0:T(128)S(1)} %get-tuple-element.13.idle_ref, s32[128]{0:T(128)S(1)} %get-tuple-element.14.single_ref, bf16[128,8,1152]{2,1,0:T(8,128)(2,1)S(1)} %all_to_all.10.back_ref, ...), custom_call_target="tpu_custom_call" | custom-call | bytes 9437184 | tf_op jit(solution)/shard_map/finish/pallas_call | solution.py:372
Async XLA Ops:
  0.6 5.6 %collective-permute-start = (f32[88,8,1024]{2,1,0:T(8,128)}, f32[88,8,1024]{2,1,0:T(8,128)S(1)}, u32[]{:S(2)}, u32[]{:S(2)}) collective-permute-start(f32[88,8,1024]{2,1,0:T(8,128)} %bitcast.8), channel_id=1, source_target_pairs={{0,128},{128,0},{1,129},{129,1},{2,130},{130,2},{3,131},{131,3},{4... | collective-permute-start | bytes 8650760 | tf_op jit(solution)/shard_map/ppermute | solution.py:391
  8.9 69.1 %all-to-all-start = ((bf16[128,8,1024]{2,1,0:T(8,128)(2,1)}), bf16[128,8,1024]{2,1,0:T(8,128)(2,1)S(1)}, u32[]{:S(2)}, u32[]{:S(2)}) async-start(bf16[128,8,1024]{2,1,0:T(8,128)(2,1)} %dispatch.1), calls=%async_computation | async-start | bytes 4194304 | tf_op jit(solution)/shard_map/all_to_all | solution.py:395
  23.9 54.1 %collective-permute-start.2 = (bf16[2,1024,512]{2,1,0:T(8,128)(2,1)}, bf16[2,1024,512]{2,1,0:T(8,128)(2,1)}, u32[]{:S(2)}, u32[]{:S(2)}) collective-permute-start(bf16[2,1024,512]{2,1,0:T(8,128)(2,1)} %bitcast.10), channel_id=1, source_target_pairs={{0,128},{128,0},{1,129},{129,1},{2,130},{130,2},{3,131},{131,3},{4... | collective-permute-start | bytes 6291464 | tf_op jit(solution)/shard_map/ppermute | solution.py:394
  78.0 4.2 %collective-permute-start.1 = (bf16[1024,1024]{1,0:T(8,128)(2,1)S(1)}, bf16[1024,1024]{1,0:T(8,128)(2,1)S(1)}, u32[]{:S(2)}, u32[]{:S(2)}) collective-permute-start(bf16[1024,1024]{1,0:T(8,128)(2,1)S(1)} %bitcast.6), channel_id=1, source_target_pairs={{0,128},{128,0},{1,129},{129,1},{2,130},{130,2},{3,131},{131,3},{4... | collective-permute-start | bytes 6291464 | tf_op jit(solution)/shard_map/ppermute | solution.py:397
  85.8 67.3 %copy-start = (f32[88,8,512]{2,1,0:T(8,128)S(1)}, f32[88,8,512]{2,1,0:T(8,128)}, u32[]{:S(2)}) copy-start(f32[88,8,512]{2,1,0:T(8,128)} %left_ref.1) | copy-start | bytes 4325380
  85.8 67.3 %copy-start.1 = (f32[88,8,512]{2,1,0:T(8,128)S(1)}, f32[88,8,512]{2,1,0:T(8,128)}, u32[]{:S(2)}) copy-start(f32[88,8,512]{2,1,0:T(8,128)} %right_ref.1) | copy-start | bytes 4325380

commit v3 on v2

--- a/solution.py
+++ b/solution.py
@@ -14,6 +14,7 @@
 WHOLE = pl.BlockSpec(memory_space=pltpu.VMEM)
 ANY = pl.BlockSpec(memory_space=pl.ANY)
 MIB = 1024 * 1024
+TILE = 512
 
 
 def in_hbm(value):
@@ -67,7 +68,7 @@
         held_ref[o] = slot + 1
         return carry
 
-    lax.fori_loop(0, blocks, place, 0, unroll=4)
+    lax.fori_loop(0, blocks, place, 0, unroll=8)
 
     def fill(o, carry):
         idles, singles, rank = carry
@@ -93,7 +94,7 @@
     zero = jnp.int32(0)
     job_ref[0] = side
     job_ref[1] = held_ref[me]
-    job_ref[2] = lax.fori_loop(0, owners, fill, (zero, zero, zero), unroll=4)[2]
+    job_ref[2] = lax.fori_loop(0, owners, fill, (zero, zero, zero), unroll=8)[2]
     copy.wait()
 
 
@@ -143,33 +144,71 @@
     )(job, send, in_vmem(mine), other)
 
 
-def fetch_kernel(*refs):
-    count = len(refs) // 2
-    sems = refs[-1]
-    copies = [pltpu.make_async_copy(refs[i], refs[count + i], sems.at[i]) for i in range(count)]
-    for copy in copies:
+def product(a, b, dims):
+    return lax.dot_general(
+        a, b, ((dims[:1], dims[1:]), ((), ())), preferred_element_type=jnp.float32
+    )
+
+
+def begin_kernel(
+    job_ref, own_ref, left_own, left_other, right_own, left_ref, right_ref, total_ref, sems
+):
+    _, width = own_ref.shape
+    half = width // 2
+    here = pl.multiple_of(job_ref[0] * half, half)
+    there = pl.multiple_of(half - job_ref[0] * half, half)
+    held = job_ref[1]
+    rights = [
+        pltpu.make_async_copy(right_own.at[slot], right_ref.at[slot], sems.at[slot])
+        for slot in range(2)
+    ]
+    lefts = [
+        pltpu.make_async_copy(source, left_ref.at[:, :, pl.ds(start, half)], sems.at[2 + i])
+        for i, (source, start) in enumerate(((left_own, here), (left_other, there)))
+    ]
+    for copy in rights + lefts:
         copy.start()
-    for copy in copies:
+    for slot in range(2):
+        rights[slot].wait()
+
+        @pl.when(held > slot)
+        def _():
+            span = pl.ds(slot * half, half)
+            for at in range(0, own_ref.shape[0], TILE):
+                rows = pl.ds(at, TILE)
+                total_ref[slot, rows, :] = product(
+                    own_ref[rows, span], right_ref[slot, pl.ds(here, half), :], (1, 0)
+                )
+
+    for copy in lefts:
         copy.wait()
 
 
-def fetch(*values):
-    size = sum(value.size * value.dtype.itemsize for value in values)
-    fetched = pl.pallas_call(
-        fetch_kernel,
-        in_specs=[ANY] * len(values),
-        out_specs=[WHOLE] * len(values),
-        out_shape=[jax.ShapeDtypeStruct(value.shape, value.dtype) for value in values],
-        scratch_shapes=[pltpu.SemaphoreType.DMA((len(values),))],
-        compiler_params=pltpu.CompilerParams(vmem_limit_bytes=16 * MIB),
-        cost_estimate=pl.CostEstimate(flops=0, bytes_accessed=2 * size, transcendentals=0),
-        name="fetch",
-    )(*[in_hbm(value) for value in values])
-    return [in_vmem(value) for value in fetched]
+def begin_updates(job, own, left_own, left_other, right_own):
+    size = own.shape[0]
+    half = size // 2
+    bf16 = jnp.bfloat16
+    begun = pl.pallas_call(
+        begin_kernel,
+        in_specs=[SMEM, WHOLE] + [ANY] * 3,
+        out_specs=[WHOLE] * 3,
+        out_shape=[
+            jax.ShapeDtypeStruct((2, size, size), bf16),
+            jax.ShapeDtypeStruct((2, size, half), bf16),
+            jax.ShapeDtypeStruct((2, size, half), jnp.float32),
+        ],
+        scratch_shapes=[pltpu.SemaphoreType.DMA((4,))],
+        compiler_params=pltpu.CompilerParams(vmem_limit_bytes=20 * MIB),
+        cost_estimate=pl.CostEstimate(
+            flops=4 * size * half * half, bytes_accessed=16 << 20, transcendentals=0
+        ),
+        name="begin",
+    )(job, own, in_hbm(left_own), in_hbm(left_other), in_hbm(right_own))
+    return [in_vmem(value) for value in begun]
 
 
 def jobs_kernel(
-    job_ref, own_ref, other_ref, left_own, left_other, right, out_ref, applied
+    job_ref, own_ref, other_ref, left, right, total_ref, out_ref, applied
 ):
     size, width = own_ref.shape
     half = width // 2
@@ -179,34 +218,28 @@
     rank = job_ref[2]
     here = pl.multiple_of(side * half, half)
     there = pl.multiple_of(half - side * half, half)
-    tile = 512
 
     def tiles(count, body):
-        for at in range(0, count, tile):
+        for at in range(0, count, TILE):
             body(at)
 
     def rows_at(start):
-        return pl.ds(pl.multiple_of(start, tile), tile)
-
-    def product(a, b, dims):
-        return lax.dot_general(
-            a, b, ((dims[:1], dims[1:]), ((), ())), preferred_element_type=jnp.float32
-        )
+        return pl.ds(pl.multiple_of(start, TILE), TILE)
 
     def update(slot):
         span = pl.ds(slot * half, half)
 
         def first(at):
             rows = rows_at(at)
-            total = product(own_ref[rows, span], right[slot, pl.ds(here, half), :], (1, 0))
-            total += product(other_ref[rows, span], right[slot, pl.ds(there, half), :], (1, 0))
+            total = product(other_ref[rows, span], right[slot, pl.ds(there, half), :], (1, 0))
+            total += total_ref[slot, rows, :]
             applied[rows, :] = total.astype(jnp.bfloat16)
 
         def second(at):
             rows = rows_at(at)
-            total = product(left_own[slot, rows, :], applied[pl.ds(here, half), :], (1, 0))
-            total += product(left_other[slot, rows, :], applied[pl.ds(there, half), :], (1, 0))
-            out_ref[rows, span] = total.astype(jnp.bfloat16)
+            out_ref[rows, span] = product(left[slot, rows, :], applied[...], (1, 0)).astype(
+                jnp.bfloat16
+            )
 
         tiles(size, first)
         tiles(size, second)
@@ -228,7 +261,7 @@
         for source, offset in ((own_ref, here), (other_ref, there)):
 
             def body(at):
-                span = pl.ds(pl.multiple_of(slot * half + at, tile), tile)
+                span = pl.ds(pl.multiple_of(slot * half + at, TILE), TILE)
                 total = product(source[:, span], own_ref[:, wanted], (0, 0))
                 out_ref[rows_at(offset + at), target] = total.astype(jnp.bfloat16)
 
@@ -271,7 +304,7 @@
         right_gram(1, start, quarter, last_part)
 
 
-def run_jobs(job, own, other, left_own, left_other, right_own):
+def run_jobs(job, own, other, left, right, total):
     size = own.shape[0]
     half = size // 2
     width = size + half // PIECES
@@ -287,7 +320,7 @@
             flops=8 * size * size * half, bytes_accessed=12 << 20, transcendentals=0
         ),
         name="jobs",
-    )(job, own, other, left_own, left_other, right_own)
+    )(job, own, other, left, right, total)
 
 
 def finish_kernel(
@@ -395,8 +428,8 @@
     arrived = lax.all_to_all(outgoing, "shard", split_axis=0, concat_axis=0, tiled=True)
     own = arrived.reshape(size, size)
     other = swapped(own)
-    roots = fetch(left_root[0], other_left, right_root[0])
-    results = run_jobs(job, own, other, *roots)
+    begun = begin_updates(job, own, left_root[0], other_left, right_root[0])
+    results = run_jobs(job, own, other, *begun)
     back = lax.all_to_all(
         results.reshape(owners, rows, -1), "shard", split_axis=0, concat_axis=0, tiled=True
     )

time: 156 us -> 156 us (level)
  no operation moved by 1% of the time
where the time goes in v3:
time: 156 us; the launch traced here: 155 us
  blocking collectives  66.9 us (43%)
  waiting for transfers between devices  55.8 us (36%)
  Pallas kernels  15.5 us (10%)
  starting transfers between devices  15.2 us (10%)
    all_to_all x1, blocking collectives, per_device(): lax.all_to_all(results.reshape(owners, rows, -1), 'shard', split_axis=0,...  66.9 us
    all_to_all x1, waiting for transfers between devices, per_device(): lax.all_to_all(outgoing, 'shard', split_axis=0, concat_axis=0, tiled=True)  54 us
    all_to_all x1, starting transfers between devices, per_device(): lax.all_to_all(outgoing, 'shard', split_axis=0, concat_axis=0, tiled=True)  15 us
    pallas_call x1, Pallas kernels, make_plan(): pl.pallas_call(plan_kernel, out_shape=[jax.ShapeDtypeStruct((n,), jnp.int...  4.42 us
    pallas_call x1, Pallas kernels, run_jobs(): pl.pallas_call(jobs_kernel, in_specs=[SMEM] + [WHOLE] * 5, out_specs=WHOL...  3.65 us
    pallas_call x1, Pallas kernels, begin_updates(): pl.pallas_call(begin_kernel, in_specs=[SMEM, WHOLE] + [ANY] * 3, out_spec...  3.45 us
  transfers between devices with their start and end apart: 4, of which 3 were waited for; matrix products, arithmetic and copies ran while one was open for 0% of the time, Pallas kernels for 5%

profile of v3, /device:TPU:32, one launch (start us, length us, event | category | flops | bytes accessed | tf_op | source)
XLA Modules:
  0.0 155.5 jit_solution(2840911966838467578)
XLA Ops:
  0.6 0.1 collective-permute-start
  0.7 4.4 %plan.1 = (s32[256]{0:T(256)S(1)}, s32[88]{0:T(128)S(1)}, s32[128]{0:T(128)S(1)}, s32[128]{0:T(128)S(1)}, s32[3]{0:T(128)S(1)}, /*index=5*/f32[88,8,512]{2,1,0:T(8,128)S(1)}) custom-call(s32[88]{0:T(128)} %owner_ref.1, f32[88,8,1024]{2,1,0:T(8,128)} %bitcast.10), custom_call_target="tpu_custom_call" | custom-call | bytes 4194304 | tf_op jit(solution)/shard_map/plan/pallas_call | solution.py:104
  5.2 1.1 collective-permute-done.other_ref
  6.2 1.3 dispatch.1
  7.5 0.0 copy-start
  7.5 1.3 copy-done
  8.9 15.0 %all-to-all-start = ((bf16[128,8,1024]{2,1,0:T(8,128)(2,1)}), bf16[128,8,1024]{2,1,0:T(8,128)(2,1)S(1)}, u32[]{:S(2)}, u32[]{:S(2)}) async-start(bf16[128,8,1024]{2,1,0:T(8,128)(2,1)} %copy-done), calls=%async_computation | async-start | bytes 4194304 | tf_op jit(solution)/shard_map/all_to_all | solution.py:428
  23.9 0.1 collective-permute-start.2
  24.0 54.0 %all-to-all-done = bf16[128,8,1024]{2,1,0:T(8,128)(2,1)S(1)} async-done(((bf16[128,8,1024]{2,1,0:T(8,128)(2,1)}), bf16[128,8,1024]{2,1,0:T(8,128)(2,1)S(1)}, u32[]{:S(2)}, u32[]{:S(2)}) %all-to-all-start) | async-done | bytes 2097184 | tf_op jit(solution)/shard_map/all_to_all | solution.py:428
  78.0 0.0 collective-permute-start.1
  78.0 0.0 collective-permute-done.2.left_other
  78.0 3.5 %begin.1 = (bf16[2,1024,1024]{2,1,0:T(8,128)(2,1)S(1)}, bf16[2,1024,512]{2,1,0:T(8,128)(2,1)S(1)}, f32[2,1024,512]{2,1,0:T(8,128)S(1)}) custom-call(s32[3]{0:T(128)S(1)} %get-tuple-element.15.job_ref, bf16[1024,1024]{1,0:T(8,128)(2,1)S(1)} %bitcast.6, bf16[2,1024,512]{2,1,0:T(8,128)(2,1)} %bitcast.12, ...), custom_call_target="tpu_custom_call" | custom-call | flops 1073741824 | bytes 16777216 | tf_op jit(solution)/shard_map/begin/pallas_call | solution.py:191
  81.5 0.7 collective-permute-done.1.other_ref
  82.2 3.7 %jobs.1 = bf16[1024,1152]{1,0:T(8,128)(2,1)S(1)} custom-call(s32[3]{0:T(128)S(1)} %get-tuple-element.15.job_ref, bf16[1024,1024]{1,0:T(8,128)(2,1)S(1)} %bitcast.7, bf16[1024,1024]{1,0:T(8,128)(2,1)S(1)} %collective-permute-done.1.other_ref, bf16[2,1024,1024]{2,1,0:T(8,128)(2,1)S(1)} %get-tuple-element.18.left, ...), custom_call_target="tpu_custom_call" | custom-call | flops 4294967296 | bytes 12582912 | tf_op jit(solution)/shard_map/jobs/pallas_call | solution.py:312
  85.8 0.0 copy-start.1
  85.8 0.0 copy-start.2
  85.8 66.9 %all_to_all.10.back_ref = bf16[128,8,1152]{2,1,0:T(8,128)(2,1)S(1)} all-to-all(bf16[128,8,1152]{2,1,0:T(8,128)(2,1)S(1)} %bitcast.8), channel_id=1, replica_groups=mesh['rep'=2,'shard'=128] {'shard'}, dimensions={0} | all-to-all | bytes 4718592 | tf_op jit(solution)/shard_map/all_to_all | solution.py:433
  152.8 0.0 copy-done.1
  152.8 0.0 copy-done.2
  152.8 2.7 %finish.1 = (f32[88,8,512]{2,1,0:T(8,128)}, f32[88,8,512]{2,1,0:T(8,128)}, bf16[88,8,512]{2,1,0:T(8,128)(2,1)}) custom-call(s32[88]{0:T(128)S(1)} %get-tuple-element.12.spot_ref, s32[128]{0:T(128)S(1)} %get-tuple-element.13.idle_ref, s32[128]{0:T(128)S(1)} %get-tuple-element.14.single_ref, bf16[128,8,1152]{2,1,0:T(8,128)(2,1)S(1)} %all_to_all.10.back_ref, ...), custom_call_target="tpu_custom_call" | custom-call | bytes 9437184 | tf_op jit(solution)/shard_map/finish/pallas_call | solution.py:405
Async XLA Ops:
  0.6 5.6 %collective-permute-start = (f32[88,8,1024]{2,1,0:T(8,128)}, f32[88,8,1024]{2,1,0:T(8,128)S(1)}, u32[]{:S(2)}, u32[]{:S(2)}) collective-permute-start(f32[88,8,1024]{2,1,0:T(8,128)} %bitcast.9), channel_id=1, source_target_pairs={{0,128},{128,0},{1,129},{129,1},{2,130},{130,2},{3,131},{131,3},{4... | collective-permute-start | bytes 8650760 | tf_op jit(solution)/shard_map/ppermute | solution.py:424
  7.5 1.3 copy-start
  8.9 69.1 %all-to-all-start = ((bf16[128,8,1024]{2,1,0:T(8,128)(2,1)}), bf16[128,8,1024]{2,1,0:T(8,128)(2,1)S(1)}, u32[]{:S(2)}, u32[]{:S(2)}) async-start(bf16[128,8,1024]{2,1,0:T(8,128)(2,1)} %copy-done), calls=%async_computation | async-start | bytes 4194304 | tf_op jit(solution)/shard_map/all_to_all | solution.py:428
  23.9 54.1 %collective-permute-start.2 = (bf16[2,1024,512]{2,1,0:T(8,128)(2,1)}, bf16[2,1024,512]{2,1,0:T(8,128)(2,1)}, u32[]{:S(2)}, u32[]{:S(2)}) collective-permute-start(bf16[2,1024,512]{2,1,0:T(8,128)(2,1)} %bitcast.11), channel_id=1, source_target_pairs={{0,128},{128,0},{1,129},{129,1},{2,130},{130,2},{3,131},{131,3},{4... | collective-permute-start | bytes 6291464 | tf_op jit(solution)/shard_map/ppermute | solution.py:427
  78.0 4.2 %collective-permute-start.1 = (bf16[1024,1024]{1,0:T(8,128)(2,1)S(1)}, bf16[1024,1024]{1,0:T(8,128)(2,1)S(1)}, u32[]{:S(2)}, u32[]{:S(2)}) collective-permute-start(bf16[1024,1024]{1,0:T(8,128)(2,1)S(1)} %bitcast.5), channel_id=1, source_target_pairs={{0,128},{128,0},{1,129},{129,1},{2,130},{130,2},{3,131},{131,3},{4... | collective-permute-start | bytes 6291464 | tf_op jit(solution)/shard_map/ppermute | solution.py:430
  85.8 66.9 %copy-start.1 = (f32[88,8,512]{2,1,0:T(8,128)S(1)}, f32[88,8,512]{2,1,0:T(8,128)}, u32[]{:S(2)}) copy-start(f32[88,8,512]{2,1,0:T(8,128)} %left_ref.1) | copy-start | bytes 4325380
  85.8 66.9 %copy-start.2 = (f32[88,8,512]{2,1,0:T(8,128)S(1)}, f32[88,8,512]{2,1,0:T(8,128)}, u32[]{:S(2)}) copy-start(f32[88,8,512]{2,1,0:T(8,128)} %right_ref.1) | copy-start | bytes 4325380

commit v4 on v3

--- a/solution.py
+++ b/solution.py
@@ -104,7 +104,9 @@
     *tables, mine = pl.pallas_call(
         plan_kernel,
         out_shape=[jax.ShapeDtypeStruct((n,), jnp.int32) for n in sizes]
-        + [jax.ShapeDtypeStruct((blocks, rows, width // 2), jnp.float32)],
+        + [
+            jax.ShapeDtypeStruct((blocks, rows, width // 2), jnp.float32),
+        ],
         in_specs=[SMEM, ANY],
         out_specs=[SMEM] * len(sizes) + [WHOLE],
         scratch_shapes=[pltpu.SMEM((owners,), jnp.int32), pltpu.SemaphoreType.DMA],
@@ -115,33 +117,58 @@
     return tables + [mine]
 
 
-def dispatch_kernel(job_ref, send_ref, mine_ref, other_ref, out_ref):
-    dests, _, width = out_ref.shape
+def room_kernel(out_ref):
+    pass
+
+
+def make_room(shape):
+    return pl.pallas_call(
+        room_kernel,
+        out_specs=ANY,
+        out_shape=jax.ShapeDtypeStruct(shape, jnp.bfloat16),
+        compiler_params=pltpu.CompilerParams(vmem_limit_bytes=60 * MIB),
+        name="room",
+    )()
+
+
+def dispatch_kernel(job_ref, send_ref, mine_ref, other_ref, _, out_ref, ready, sems):
+    dests, _, width = ready.shape
     half = width // 2
     here = pl.ds(pl.multiple_of(job_ref[0] * half, half), half)
+    steps = sems.shape[0]
+    count = dests // steps
 
     def one(dest, carry):
         for slot in range(2):
             b = send_ref[2 * dest + slot]
-            out_ref[dest, :, slot * half : (slot + 1) * half] = (
+            ready[dest, :, slot * half : (slot + 1) * half] = (
                 mine_ref[b] + other_ref[b, :, here]
             ).astype(jnp.bfloat16)
         return carry
 
-    lax.fori_loop(0, dests, one, 0, unroll=4)
-
-
-def dispatch(job, send, mine, other, owners):
-    _, rows, width = other.shape
+    copies = []
+    for step in range(steps):
+        lax.fori_loop(step * count, (step + 1) * count, one, 0, unroll=4)
+        part = pl.ds(step * count, count)
+        copies.append(pltpu.make_async_copy(ready.at[part], out_ref.at[part], sems.at[step]))
+        copies[-1].start()
+    for copy in copies:
+        copy.wait()
+
+
+def dispatch(job, send, mine, other, room):
+    shape = room.shape
     return pl.pallas_call(
         dispatch_kernel,
-        in_specs=[SMEM, SMEM, WHOLE, WHOLE],
-        out_specs=WHOLE,
-        out_shape=jax.ShapeDtypeStruct((owners, rows, width), jnp.bfloat16),
+        in_specs=[SMEM, SMEM, WHOLE, WHOLE, ANY],
+        out_specs=ANY,
+        out_shape=jax.ShapeDtypeStruct(shape, jnp.bfloat16),
+        input_output_aliases={4: 0},
+        scratch_shapes=[pltpu.VMEM(shape, jnp.bfloat16), pltpu.SemaphoreType.DMA((4,))],
         compiler_params=pltpu.CompilerParams(vmem_limit_bytes=16 * MIB),
         cost_estimate=pl.CostEstimate(flops=0, bytes_accessed=5 << 20, transcendentals=0),
         name="dispatch",
-    )(job, send, in_vmem(mine), other)
+    )(job, send, in_vmem(mine), other, in_hbm(room))
 
 
 def product(a, b, dims):
@@ -226,23 +253,26 @@
     def rows_at(start):
         return pl.ds(pl.multiple_of(start, TILE), TILE)
 
-    def update(slot):
+    def right_half(slot):
         span = pl.ds(slot * half, half)
 
-        def first(at):
+        def body(at):
             rows = rows_at(at)
             total = product(other_ref[rows, span], right[slot, pl.ds(there, half), :], (1, 0))
-            total += total_ref[slot, rows, :]
-            applied[rows, :] = total.astype(jnp.bfloat16)
-
-        def second(at):
+            applied[slot, rows, :] = (total + total_ref[slot, rows, :]).astype(jnp.bfloat16)
+
+        tiles(size, body)
+
+    def left_half(slot):
+        span = pl.ds(slot * half, half)
+
+        def body(at):
             rows = rows_at(at)
-            out_ref[rows, span] = product(left[slot, rows, :], applied[...], (1, 0)).astype(
+            out_ref[rows, span] = product(left[slot, rows, :], applied[slot], (1, 0)).astype(
                 jnp.bfloat16
             )
 
-        tiles(size, first)
-        tiles(size, second)
+        tiles(size, body)
 
     def left_gram(slot, start, count, target):
         span = pl.ds(slot * half, half)
@@ -271,26 +301,31 @@
     second_part = pl.ds(half, half)
     last_part = pl.ds(width, quarter)
 
-    @pl.when(held > 0)
-    def _():
-        update(0)
+    @pl.when(held == 2)
+    def _():
+        right_half(0)
+        right_half(1)
+        left_half(0)
+        left_half(1)
+
+    @pl.when(held == 1)
+    def _():
+        right_half(0)
 
     @pl.when(held == 0)
     def _():
         left_gram(0, 0, half, first_part)
         right_gram(0, 0, half, second_part)
 
-    @pl.when(held == 2)
-    def _():
-        update(1)
-
     @pl.when((held == 1) & (rank % 2 == 0))
     def _():
         left_gram(1, 0, half, second_part)
+        left_half(0)
 
     @pl.when((held == 1) & (rank % 2 == 1))
     def _():
         right_gram(1, 0, half, second_part)
+        left_half(0)
 
     piece = rank % (2 * PIECES)
     start = (piece % PIECES) * quarter
@@ -314,7 +349,7 @@
         in_specs=[SMEM] + [WHOLE] * 5,
         out_specs=WHOLE,
         out_shape=jax.ShapeDtypeStruct((size, width), bf16),
-        scratch_shapes=[pltpu.VMEM((size, half), bf16)],
+        scratch_shapes=[pltpu.VMEM((2, size, half), bf16)],
         compiler_params=pltpu.CompilerParams(vmem_limit_bytes=20 * MIB),
         cost_estimate=pl.CostEstimate(
             flops=8 * size * size * half, bytes_accessed=12 << 20, transcendentals=0
@@ -423,7 +458,8 @@
     gradient = gradients[0]
     other_gradient = swapped(gradient)
     send, spot, idle, single, job, mine = make_plan(block_owner, gradient, owners)
-    outgoing = dispatch(job, send, mine, other_gradient, owners)
+    room = make_room((owners, rows, size))
+    outgoing = dispatch(job, send, mine, other_gradient, room)
     other_left = swapped(left_root[0])
     arrived = lax.all_to_all(outgoing, "shard", split_axis=0, concat_axis=0, tiled=True)
     own = arrived.reshape(size, size)

time: 156 us -> 156 us (level)
  no operation moved by 1% of the time
where the time goes in v4:
time: 156 us; the launch traced here: 155 us
  blocking collectives  66 us (42%)
  waiting for transfers between devices  55.8 us (36%)
  Pallas kernels  17 us (11%)
  starting transfers between devices  15.2 us (10%)
    all_to_all x1, blocking collectives, per_device(): lax.all_to_all(results.reshape(owners, rows, -1), 'shard', split_axis=0,...  66 us
    all_to_all x1, waiting for transfers between devices, per_device(): lax.all_to_all(outgoing, 'shard', split_axis=0, concat_axis=0, tiled=True)  54 us
    all_to_all x1, starting transfers between devices, per_device(): lax.all_to_all(outgoing, 'shard', split_axis=0, concat_axis=0, tiled=True)  15 us
    pallas_call x1, Pallas kernels, make_plan(): pl.pallas_call(plan_kernel, out_shape=[jax.ShapeDtypeStruct((n,), jnp.int...  4.42 us
    pallas_call x1, Pallas kernels, run_jobs(): pl.pallas_call(jobs_kernel, in_specs=[SMEM] + [WHOLE] * 5, out_specs=WHOL...  4.19 us
    pallas_call x1, Pallas kernels, begin_updates(): pl.pallas_call(begin_kernel, in_specs=[SMEM, WHOLE] + [ANY] * 3, out_spec...  3.45 us
  transfers between devices with their start and end apart: 4, of which 3 were waited for; matrix products, arithmetic and copies ran while one was open for 0% of the time, Pallas kernels for 5%

profile of v4, /device:TPU:32, one launch (start us, length us, event | category | flops | bytes accessed | tf_op | source)
XLA Modules:
  0.0 154.9 jit_solution(15398903948541040817)
XLA Ops:
  0.6 0.1 collective-permute-start
  0.7 4.4 %plan.1 = (s32[256]{0:T(256)S(1)}, s32[88]{0:T(128)S(1)}, s32[128]{0:T(128)S(1)}, s32[128]{0:T(128)S(1)}, s32[3]{0:T(128)S(1)}, /*index=5*/f32[88,8,512]{2,1,0:T(8,128)S(1)}) custom-call(s32[88]{0:T(128)} %owner_ref.1, f32[88,8,1024]{2,1,0:T(8,128)} %bitcast.10), custom_call_target="tpu_custom_call" | custom-call | bytes 4194304 | tf_op jit(solution)/shard_map/plan/pallas_call | solution.py:104
  5.2 1.0 collective-permute-done.other_ref
  6.2 2.2 %dispatch.1 = bf16[128,8,1024]{2,1,0:T(8,128)(2,1)} custom-call(s32[3]{0:T(128)S(1)} %get-tuple-element.15.job_ref, s32[256]{0:T(256)S(1)} %get-tuple-element.16.send_ref, f32[88,8,512]{2,1,0:T(8,128)S(1)} %get-tuple-element.17.mine_ref, f32[88,8,1024]{2,1,0:T(8,128)S(1)} %collective-permute-done.other_ref, ...), custom_call_target="tpu_custom_call", output_to_operand_aliasing={{}: (4, {})} | custom-call | bytes 5242880 | tf_op jit(solution)/shard_map/dispatch/pallas_call | solution.py:161
  8.4 15.0 %all-to-all-start = ((bf16[128,8,1024]{2,1,0:T(8,128)(2,1)}), bf16[128,8,1024]{2,1,0:T(8,128)(2,1)S(1)}, u32[]{:S(2)}, u32[]{:S(2)}) async-start(bf16[128,8,1024]{2,1,0:T(8,128)(2,1)} %dispatch.1), calls=%async_computation | async-start | bytes 4194304 | tf_op jit(solution)/shard_map/all_to_all | solution.py:464
  23.4 0.1 collective-permute-start.2
  23.5 54.0 %all-to-all-done = bf16[128,8,1024]{2,1,0:T(8,128)(2,1)S(1)} async-done(((bf16[128,8,1024]{2,1,0:T(8,128)(2,1)}), bf16[128,8,1024]{2,1,0:T(8,128)(2,1)S(1)}, u32[]{:S(2)}, u32[]{:S(2)}) %all-to-all-start) | async-done | bytes 2097184 | tf_op jit(solution)/shard_map/all_to_all | solution.py:464
  77.6 0.0 collective-permute-start.1
  77.6 0.0 collective-permute-done.2.left_other
  77.6 3.5 %begin.1 = (bf16[2,1024,1024]{2,1,0:T(8,128)(2,1)S(1)}, bf16[2,1024,512]{2,1,0:T(8,128)(2,1)S(1)}, f32[2,1024,512]{2,1,0:T(8,128)S(1)}) custom-call(s32[3]{0:T(128)S(1)} %get-tuple-element.15.job_ref, bf16[1024,1024]{1,0:T(8,128)(2,1)S(1)} %bitcast.6, bf16[2,1024,512]{2,1,0:T(8,128)(2,1)} %bitcast.12, ...), custom_call_target="tpu_custom_call" | custom-call | flops 1073741824 | bytes 16777216 | tf_op jit(solution)/shard_map/begin/pallas_call | solution.py:218
  81.0 0.7 collective-permute-done.1.other_ref
  81.7 4.2 %jobs.1 = bf16[1024,1152]{1,0:T(8,128)(2,1)S(1)} custom-call(s32[3]{0:T(128)S(1)} %get-tuple-element.15.job_ref, bf16[1024,1024]{1,0:T(8,128)(2,1)S(1)} %bitcast.7, bf16[1024,1024]{1,0:T(8,128)(2,1)S(1)} %collective-permute-done.1.other_ref, bf16[2,1024,1024]{2,1,0:T(8,128)(2,1)S(1)} %get-tuple-element.18.left, ...), custom_call_target="tpu_custom_call" | custom-call | flops 4294967296 | bytes 12582912 | tf_op jit(solution)/shard_map/jobs/pallas_call | solution.py:347
  85.9 0.0 copy-start
  85.9 0.0 copy-start.1
  85.9 66.0 %all_to_all.10.back_ref = bf16[128,8,1152]{2,1,0:T(8,128)(2,1)S(1)} all-to-all(bf16[128,8,1152]{2,1,0:T(8,128)(2,1)S(1)} %bitcast.8), channel_id=1, replica_groups=mesh['rep'=2,'shard'=128] {'shard'}, dimensions={0} | all-to-all | bytes 4718592 | tf_op jit(solution)/shard_map/all_to_all | solution.py:469
  152.0 0.0 copy-done
  152.0 0.0 copy-done.1
  152.0 2.7 %finish.1 = (f32[88,8,512]{2,1,0:T(8,128)}, f32[88,8,512]{2,1,0:T(8,128)}, bf16[88,8,512]{2,1,0:T(8,128)(2,1)}) custom-call(s32[88]{0:T(128)S(1)} %get-tuple-element.12.spot_ref, s32[128]{0:T(128)S(1)} %get-tuple-element.13.idle_ref, s32[128]{0:T(128)S(1)} %get-tuple-element.14.single_ref, bf16[128,8,1152]{2,1,0:T(8,128)(2,1)S(1)} %all_to_all.10.back_ref, ...), custom_call_target="tpu_custom_call" | custom-call | bytes 9437184 | tf_op jit(solution)/shard_map/finish/pallas_call | solution.py:440
  (1 shorter events, 0.0 us)
Async XLA Ops:
  0.6 5.6 %collective-permute-start = (f32[88,8,1024]{2,1,0:T(8,128)}, f32[88,8,1024]{2,1,0:T(8,128)S(1)}, u32[]{:S(2)}, u32[]{:S(2)}) collective-permute-start(f32[88,8,1024]{2,1,0:T(8,128)} %bitcast.9), channel_id=1, source_target_pairs={{0,128},{128,0},{1,129},{129,1},{2,130},{130,2},{3,131},{131,3},{4... | collective-permute-start | bytes 8650760 | tf_op jit(solution)/shard_map/ppermute | solution.py:459
  8.4 69.2 %all-to-all-start = ((bf16[128,8,1024]{2,1,0:T(8,128)(2,1)}), bf16[128,8,1024]{2,1,0:T(8,128)(2,1)S(1)}, u32[]{:S(2)}, u32[]{:S(2)}) async-start(bf16[128,8,1024]{2,1,0:T(8,128)(2,1)} %dispatch.1), calls=%async_computation | async-start | bytes 4194304 | tf_op jit(solution)/shard_map/all_to_all | solution.py:464
  23.4 54.1 %collective-permute-start.2 = (bf16[2,1024,512]{2,1,0:T(8,128)(2,1)}, bf16[2,1024,512]{2,1,0:T(8,128)(2,1)}, u32[]{:S(2)}, u32[]{:S(2)}) collective-permute-start(bf16[2,1024,512]{2,1,0:T(8,128)(2,1)} %bitcast.11), channel_id=1, source_target_pairs={{0,128},{128,0},{1,129},{129,1},{2,130},{130,2},{3,131},{131,3},{4... | collective-permute-start | bytes 6291464 | tf_op jit(solution)/shard_map/ppermute | solution.py:463
  77.6 4.2 %collective-permute-start.1 = (bf16[1024,1024]{1,0:T(8,128)(2,1)S(1)}, bf16[1024,1024]{1,0:T(8,128)(2,1)S(1)}, u32[]{:S(2)}, u32[]{:S(2)}) collective-permute-start(bf16[1024,1024]{1,0:T(8,128)(2,1)S(1)} %bitcast.5), channel_id=1, source_target_pairs={{0,128},{128,0},{1,129},{129,1},{2,130},{130,2},{3,131},{131,3},{4... | collective-permute-start | bytes 6291464 | tf_op jit(solution)/shard_map/ppermute | solution.py:466
  85.9 66.1 %copy-start = (f32[88,8,512]{2,1,0:T(8,128)S(1)}, f32[88,8,512]{2,1,0:T(8,128)}, u32[]{:S(2)}) copy-start(f32[88,8,512]{2,1,0:T(8,128)} %left_ref.1) | copy-start | bytes 4325380
  85.9 66.1 %copy-start.1 = (f32[88,8,512]{2,1,0:T(8,128)S(1)}, f32[88,8,512]{2,1,0:T(8,128)}, u32[]{:S(2)}) copy-start(f32[88,8,512]{2,1,0:T(8,128)} %right_ref.1) | copy-start | bytes 4325380

commit v5 on v4

--- a/solution.py
+++ b/solution.py
@@ -14,7 +14,7 @@
 WHOLE = pl.BlockSpec(memory_space=pltpu.VMEM)
 ANY = pl.BlockSpec(memory_space=pl.ANY)
 MIB = 1024 * 1024
-TILE = 512
+TILE = 1024
 
 
 def in_hbm(value):
@@ -290,12 +290,12 @@
         wanted = pl.ds(pl.multiple_of(slot * half + start, quarter), count)
         for source, offset in ((own_ref, here), (other_ref, there)):
 
-            def body(at):
-                span = pl.ds(pl.multiple_of(slot * half + at, TILE), TILE)
+            def body():
+                span = pl.ds(pl.multiple_of(slot * half, half), half)
                 total = product(source[:, span], own_ref[:, wanted], (0, 0))
-                out_ref[rows_at(offset + at), target] = total.astype(jnp.bfloat16)
-
-            tiles(half, body)
+                out_ref[pl.ds(offset, half), target] = total.astype(jnp.bfloat16)
+
+            body()
 
     first_part = pl.ds(0, half)
     second_part = pl.ds(half, half)
@@ -423,10 +423,10 @@
             copy.start()
             copies.append(copy)
 
-    third = idle_blocks // 3
-    for first in range(0, idle_blocks, third):
-        lax.fori_loop(first, first + third, whole_pair, 0, unroll=2)
-        send(first, first + third)
+    step = idle_blocks // 4
+    for first in range(0, idle_blocks, step):
+        lax.fori_loop(first, first + step, whole_pair, 0, unroll=2)
+        send(first, first + step)
     lax.fori_loop(idle_blocks, split_from, shared_pair, 0, unroll=2)
     lax.fori_loop(split_from, blocks, split_pair, 0)
     send(idle_blocks, blocks)
@@ -443,7 +443,7 @@
         out_specs=[ANY] * 3,
         out_shape=[jax.ShapeDtypeStruct(shape, kind) for kind in kinds],
         scratch_shapes=[pltpu.VMEM(shape, kind) for kind in kinds]
-        + [pltpu.SemaphoreType.DMA((12,))],
+        + [pltpu.SemaphoreType.DMA((15,))],
         compiler_params=pltpu.CompilerParams(vmem_limit_bytes=16 * MIB),
         cost_estimate=pl.CostEstimate(flops=0, bytes_accessed=9 << 20, transcendentals=0),
         name="finish",

time: 156 us -> 156 us (level)
  no operation moved by 1% of the time
where the time goes in v5:
time: 156 us; the launch traced here: 155 us
  blocking collectives  66.4 us (43%)
  waiting for transfers between devices  55.8 us (36%)
  Pallas kernels  16.6 us (11%)
  starting transfers between devices  15.2 us (10%)
    all_to_all x1, blocking collectives, per_device(): lax.all_to_all(results.reshape(owners, rows, -1), 'shard', split_axis=0,...  66.4 us
    all_to_all x1, waiting for transfers between devices, per_device(): lax.all_to_all(outgoing, 'shard', split_axis=0, concat_axis=0, tiled=True)  54 us
    all_to_all x1, starting transfers between devices, per_device(): lax.all_to_all(outgoing, 'shard', split_axis=0, concat_axis=0, tiled=True)  15 us
    pallas_call x1, Pallas kernels, make_plan(): pl.pallas_call(plan_kernel, out_shape=[jax.ShapeDtypeStruct((n,), jnp.int...  4.42 us
    pallas_call x1, Pallas kernels, run_jobs(): pl.pallas_call(jobs_kernel, in_specs=[SMEM] + [WHOLE] * 5, out_specs=WHOL...  3.83 us
    pallas_call x1, Pallas kernels, begin_updates(): pl.pallas_call(begin_kernel, in_specs=[SMEM, WHOLE] + [ANY] * 3, out_spec...  3.45 us
  transfers between devices with their start and end apart: 4, of which 3 were waited for; matrix products, arithmetic and copies ran while one was open for 0% of the time, Pallas kernels for 5%

profile of v5, /device:TPU:32, one launch (start us, length us, event | category | flops | bytes accessed | tf_op | source)
XLA Modules:
  0.0 154.8 jit_solution(6931932861301417967)
XLA Ops:
  0.6 0.1 collective-permute-start
  0.7 4.4 %plan.1 = (s32[256]{0:T(256)S(1)}, s32[88]{0:T(128)S(1)}, s32[128]{0:T(128)S(1)}, s32[128]{0:T(128)S(1)}, s32[3]{0:T(128)S(1)}, /*index=5*/f32[88,8,512]{2,1,0:T(8,128)S(1)}) custom-call(s32[88]{0:T(128)} %owner_ref.1, f32[88,8,1024]{2,1,0:T(8,128)} %bitcast.10), custom_call_target="tpu_custom_call" | custom-call | bytes 4194304 | tf_op jit(solution)/shard_map/plan/pallas_call | solution.py:104
  5.2 1.0 collective-permute-done.other_ref
  6.2 2.2 %dispatch.1 = bf16[128,8,1024]{2,1,0:T(8,128)(2,1)} custom-call(s32[3]{0:T(128)S(1)} %get-tuple-element.15.job_ref, s32[256]{0:T(256)S(1)} %get-tuple-element.16.send_ref, f32[88,8,512]{2,1,0:T(8,128)S(1)} %get-tuple-element.17.mine_ref, f32[88,8,1024]{2,1,0:T(8,128)S(1)} %collective-permute-done.other_ref, ...), custom_call_target="tpu_custom_call", output_to_operand_aliasing={{}: (4, {})} | custom-call | bytes 5242880 | tf_op jit(solution)/shard_map/dispatch/pallas_call | solution.py:161
  8.4 15.0 %all-to-all-start = ((bf16[128,8,1024]{2,1,0:T(8,128)(2,1)}), bf16[128,8,1024]{2,1,0:T(8,128)(2,1)S(1)}, u32[]{:S(2)}, u32[]{:S(2)}) async-start(bf16[128,8,1024]{2,1,0:T(8,128)(2,1)} %dispatch.1), calls=%async_computation | async-start | bytes 4194304 | tf_op jit(solution)/shard_map/all_to_all | solution.py:464
  23.4 0.1 collective-permute-start.2
  23.5 54.0 %all-to-all-done = bf16[128,8,1024]{2,1,0:T(8,128)(2,1)S(1)} async-done(((bf16[128,8,1024]{2,1,0:T(8,128)(2,1)}), bf16[128,8,1024]{2,1,0:T(8,128)(2,1)S(1)}, u32[]{:S(2)}, u32[]{:S(2)}) %all-to-all-start) | async-done | bytes 2097184 | tf_op jit(solution)/shard_map/all_to_all | solution.py:464
  77.6 0.0 collective-permute-start.1
  77.6 0.0 collective-permute-done.2.left_other
  77.6 3.5 %begin.1 = (bf16[2,1024,1024]{2,1,0:T(8,128)(2,1)S(1)}, bf16[2,1024,512]{2,1,0:T(8,128)(2,1)S(1)}, f32[2,1024,512]{2,1,0:T(8,128)S(1)}) custom-call(s32[3]{0:T(128)S(1)} %get-tuple-element.15.job_ref, bf16[1024,1024]{1,0:T(8,128)(2,1)S(1)} %bitcast.6, bf16[2,1024,512]{2,1,0:T(8,128)(2,1)} %bitcast.12, ...), custom_call_target="tpu_custom_call" | custom-call | flops 1073741824 | bytes 16777216 | tf_op jit(solution)/shard_map/begin/pallas_call | solution.py:218
  81.0 0.7 collective-permute-done.1.other_ref
  81.7 3.8 %jobs.1 = bf16[1024,1152]{1,0:T(8,128)(2,1)S(1)} custom-call(s32[3]{0:T(128)S(1)} %get-tuple-element.15.job_ref, bf16[1024,1024]{1,0:T(8,128)(2,1)S(1)} %bitcast.7, bf16[1024,1024]{1,0:T(8,128)(2,1)S(1)} %collective-permute-done.1.other_ref, bf16[2,1024,1024]{2,1,0:T(8,128)(2,1)S(1)} %get-tuple-element.18.left, ...), custom_call_target="tpu_custom_call" | custom-call | flops 4294967296 | bytes 12582912 | tf_op jit(solution)/shard_map/jobs/pallas_call | solution.py:347
  85.6 0.0 copy-start
  85.6 0.0 copy-start.1
  85.6 66.4 %all_to_all.10.back_ref = bf16[128,8,1152]{2,1,0:T(8,128)(2,1)S(1)} all-to-all(bf16[128,8,1152]{2,1,0:T(8,128)(2,1)S(1)} %bitcast.8), channel_id=1, replica_groups=mesh['rep'=2,'shard'=128] {'shard'}, dimensions={0} | all-to-all | bytes 4718592 | tf_op jit(solution)/shard_map/all_to_all | solution.py:469
  152.0 0.0 copy-done
  152.0 0.0 copy-done.1
  152.0 2.7 %finish.1 = (f32[88,8,512]{2,1,0:T(8,128)}, f32[88,8,512]{2,1,0:T(8,128)}, bf16[88,8,512]{2,1,0:T(8,128)(2,1)}) custom-call(s32[88]{0:T(128)S(1)} %get-tuple-element.12.spot_ref, s32[128]{0:T(128)S(1)} %get-tuple-element.13.idle_ref, s32[128]{0:T(128)S(1)} %get-tuple-element.14.single_ref, bf16[128,8,1152]{2,1,0:T(8,128)(2,1)S(1)} %all_to_all.10.back_ref, ...), custom_call_target="tpu_custom_call" | custom-call | bytes 9437184 | tf_op jit(solution)/shard_map/finish/pallas_call | solution.py:440
  (1 shorter events, 0.0 us)
Async XLA Ops:
  0.6 5.6 %collective-permute-start = (f32[88,8,1024]{2,1,0:T(8,128)}, f32[88,8,1024]{2,1,0:T(8,128)S(1)}, u32[]{:S(2)}, u32[]{:S(2)}) collective-permute-start(f32[88,8,1024]{2,1,0:T(8,128)} %bitcast.9), channel_id=1, source_target_pairs={{0,128},{128,0},{1,129},{129,1},{2,130},{130,2},{3,131},{131,3},{4... | collective-permute-start | bytes 8650760 | tf_op jit(solution)/shard_map/ppermute | solution.py:459
  8.4 69.2 %all-to-all-start = ((bf16[128,8,1024]{2,1,0:T(8,128)(2,1)}), bf16[128,8,1024]{2,1,0:T(8,128)(2,1)S(1)}, u32[]{:S(2)}, u32[]{:S(2)}) async-start(bf16[128,8,1024]{2,1,0:T(8,128)(2,1)} %dispatch.1), calls=%async_computation | async-start | bytes 4194304 | tf_op jit(solution)/shard_map/all_to_all | solution.py:464
  23.4 54.1 %collective-permute-start.2 = (bf16[2,1024,512]{2,1,0:T(8,128)(2,1)}, bf16[2,1024,512]{2,1,0:T(8,128)(2,1)}, u32[]{:S(2)}, u32[]{:S(2)}) collective-permute-start(bf16[2,1024,512]{2,1,0:T(8,128)(2,1)} %bitcast.11), channel_id=1, source_target_pairs={{0,128},{128,0},{1,129},{129,1},{2,130},{130,2},{3,131},{131,3},{4... | collective-permute-start | bytes 6291464 | tf_op jit(solution)/shard_map/ppermute | solution.py:463
  77.6 4.2 %collective-permute-start.1 = (bf16[1024,1024]{1,0:T(8,128)(2,1)S(1)}, bf16[1024,1024]{1,0:T(8,128)(2,1)S(1)}, u32[]{:S(2)}, u32[]{:S(2)}) collective-permute-start(bf16[1024,1024]{1,0:T(8,128)(2,1)S(1)} %bitcast.5), channel_id=1, source_target_pairs={{0,128},{128,0},{1,129},{129,1},{2,130},{130,2},{3,131},{131,3},{4... | collective-permute-start | bytes 6291464 | tf_op jit(solution)/shard_map/ppermute | solution.py:466
  85.6 66.4 %copy-start = (f32[88,8,512]{2,1,0:T(8,128)S(1)}, f32[88,8,512]{2,1,0:T(8,128)}, u32[]{:S(2)}) copy-start(f32[88,8,512]{2,1,0:T(8,128)} %left_ref.1) | copy-start | bytes 4325380
  85.6 66.4 %copy-start.1 = (f32[88,8,512]{2,1,0:T(8,128)S(1)}, f32[88,8,512]{2,1,0:T(8,128)}, u32[]{:S(2)}) copy-start(f32[88,8,512]{2,1,0:T(8,128)} %right_ref.1) | copy-start | bytes 4325380
